TPU v7x, 256 devices: a whole 4x4x8 slice. The times are simulated.
256 devices in a mesh: seq: 32 (over x, z), head: 8 (over y, core).
Axes of the slice: x: 4, y: 4, z: 8, core: 2. Of those that a mesh axis runs over, the one named last changes fastest.
Arguments:
- queries: bfloat16 [4096, 4096], P('seq', 'head'), may hold values from -6 to 6
- key_vecs: bfloat16 [4096, 3, 4096], P('seq', None, 'head'), as said below
- values: bfloat16 [4096, 3, 4096], P('seq', None, 'head'), may hold values from -6 to 6
- out_gate: bfloat16 [4096, 4096], P('seq', 'head'), may hold values from -6 to 6
- beta_rates: float32 [3, 32, 4096], P(None, 'head', 'seq'), may hold values from 0 to 2
- log_decay: float32 [32, 4096], P('head', 'seq')
- norm_gain: float32 [128], replicated, may hold values from 0.1 to 1.9
- w_out: bfloat16 [4096, 4096], P('head'), may hold values from -0.09375 to 0.09375
Outputs:
- layer_out: bfloat16 [4096, 4096], P(('seq', 'head'))
Inputs may be any that keep to these rules, and one draw needn't show every extreme that they name: `key_vecs`: each aligned block of 128 entries is one key.
All inputs are finite; a program needn't handle non-finite values.
Results may differ from a plain program's by a relative error of at most 0.0059.
Values sent between devices are 32-bit elements; how exact they have to be, the bound alone decides.
A program may use at most 64 MiB of HBM per device.

v0:
```python
import jax
import jax.numpy as jnp
from jax import lax
from jax.sharding import PartitionSpec as P

GROUP = 64


full_precision = lax.Precision.HIGHEST


def shifted(value, axis, by):
    length = lax.axis_size(axis)
    pairs = [(i, i + by) for i in range(length) if 0 <= i + by < length]
    return lax.ppermute(value, axis, pairs)


def chain_product(left_mat, right_mat):
    return jnp.einsum("hde,hef->hdf", left_mat, right_mat, precision=full_precision)


def on_device(queries, key_vecs, values, out_gate, beta_rates, log_decay, norm_gain, w_out):
    step_count = beta_rates.shape[0]
    head_count = beta_rates.shape[1]
    length = queries.shape[0]
    head_width = queries.shape[1] // head_count
    blocks = length // GROUP
    micro_len = step_count * GROUP
    query_rows = (
        queries.astype(jnp.float32)
        .reshape(blocks, GROUP, head_count, head_width)
        .transpose(2, 0, 1, 3)
    )
    raw_keys = key_vecs.astype(jnp.float32).reshape(
        blocks, GROUP, step_count, head_count, head_width
    )
    unit_keys = raw_keys / jnp.sqrt(jnp.sum(raw_keys * raw_keys, -1, keepdims=True) + 1e-06)
    unit_keys = unit_keys.transpose(3, 0, 1, 2, 4).reshape(
        head_count, blocks, micro_len, head_width
    )
    value_rows = values.astype(jnp.float32).reshape(
        blocks, GROUP, step_count, head_count, head_width
    )
    value_rows = value_rows.transpose(3, 0, 1, 2, 4).reshape(
        head_count, blocks, micro_len, head_width
    )
    strength = (
        beta_rates.reshape(step_count, head_count, blocks, GROUP)
        .transpose(1, 2, 3, 0)
        .reshape(head_count, blocks, micro_len)
    )
    token_decay = log_decay.reshape(head_count, blocks, GROUP, 1)
    micro_decay = jnp.concatenate(
        [token_decay, jnp.zeros((head_count, blocks, GROUP, step_count - 1), jnp.float32)], -1
    )
    running_log = jnp.cumsum(micro_decay.reshape(head_count, blocks, micro_len), -1)
    token_places = jnp.arange(micro_len)
    below_diag = token_places[:, None] > token_places[None, :]
    log_gap = running_log[..., :, None] - running_log[..., None, :]
    decay_ratio = jnp.where(below_diag, jnp.exp(jnp.where(below_diag, log_gap, 0.0)), 0.0)
    key_gram = jnp.einsum("hcmd,hcid->hcmi", unit_keys, unit_keys, precision=full_precision)
    system = jnp.eye(micro_len, dtype=jnp.float32) + strength[..., :, None] * decay_ratio * key_gram
    right_side = jnp.concatenate(
        [
            strength[..., None] * value_rows,
            (strength * jnp.exp(running_log))[..., None] * unit_keys,
        ],
        -1,
    )
    solved = jax.scipy.linalg.solve_triangular(system, right_side, lower=True, unit_diagonal=True)
    value_part = solved[..., :head_width]
    key_part = solved[..., head_width:]
    end_log = running_log[..., -1:]
    tail_decay = jnp.exp(end_log - running_log)[..., None]
    eye_small = jnp.eye(head_width, dtype=jnp.float32)
    transit = jnp.exp(end_log)[..., None] * eye_small - jnp.einsum(
        "hcmd,hcme->hcde", unit_keys, tail_decay * key_part, precision=full_precision
    )
    inflow = jnp.einsum(
        "hcmd,hcme->hcde", unit_keys, tail_decay * value_part, precision=full_precision
    )
    last_micro = jnp.arange(GROUP) * step_count + step_count - 1
    visible = token_places[None, :] <= last_micro[:, None]
    query_log = running_log[..., step_count - 1 :: step_count]
    query_gap = query_log[..., :, None] - running_log[..., None, :]
    scores = jnp.einsum("hctd,hcmd->hctm", query_rows, unit_keys, precision=full_precision)
    scores = scores * jnp.where(visible, jnp.exp(jnp.where(visible, query_gap, 0.0)), 0.0)
    local_out = jnp.einsum("hctm,hcme->hcte", scores, value_part, precision=full_precision)
    local_query = jnp.exp(query_log)[..., None] * query_rows - jnp.einsum(
        "hctm,hcme->hcte", scores, key_part, precision=full_precision
    )
    transit_seq = transit.transpose(1, 0, 2, 3)
    inflow_seq = inflow.transpose(1, 0, 2, 3)
    local_out_seq = local_out.transpose(1, 0, 2, 3)
    local_query_seq = local_query.transpose(1, 0, 2, 3)
    identity_map = jnp.broadcast_to(eye_small, (head_count, head_width, head_width))
    empty_state = jnp.zeros((head_count, head_width, head_width), jnp.float32)

    def compose(running, block_item):
        block_map, block_flow = block_item
        return (
            (
                chain_product(block_map, running[0]),
                chain_product(block_map, running[1]) + block_flow,
            ),
            None,
        )

    device_pair, nothing = lax.scan(compose, (identity_map, empty_state), (transit_seq, inflow_seq))
    device_map, device_flow = device_pair

    def relay(relay_turn, relay_pair):
        arrived = shifted(relay_pair[1], "seq", 1)
        return (arrived, chain_product(device_map, arrived) + device_flow)

    relay_pair = lax.fori_loop(0, lax.axis_size("seq") - 1, relay, (empty_state, device_flow))
    incoming = relay_pair[0]

    def replay(state_now, block_item):
        block_map, block_flow, block_out, block_query = block_item
        emitted = block_out + jnp.einsum(
            "htd,hde->hte", block_query, state_now, precision=full_precision
        )
        return (chain_product(block_map, state_now) + block_flow, emitted)

    final_state, head_out = lax.scan(
        replay, incoming, (transit_seq, inflow_seq, local_out_seq, local_query_seq)
    )
    head_out = head_out.transpose(0, 2, 1, 3).reshape(length, head_count, head_width)
    mean_square = jnp.mean(head_out * head_out, -1, keepdims=True)
    normed = head_out / jnp.sqrt(mean_square + 1e-05) * norm_gain
    gate_rows = out_gate.astype(jnp.float32).reshape(length, head_count, head_width)
    gated = (
        (normed * jax.nn.silu(gate_rows))
        .reshape(length, head_count * head_width)
        .astype(jnp.bfloat16)
    )
    summed = lax.psum_scatter(
        jnp.dot(gated, w_out, preferred_element_type=jnp.float32),
        "head",
        scatter_dimension=0,
        tiled=True,
    )
    return summed.astype(jnp.bfloat16)


def solution(mesh):
    placed = (
        P("seq", "head"),
        P("seq", None, "head"),
        P("seq", None, "head"),
        P("seq", "head"),
        P(None, "head", "seq"),
        P("head", "seq"),
        P(),
        P("head", None),
    )
    return jax.shard_map(
        on_device, mesh=mesh, in_specs=placed, out_specs=P(("seq", "head"), None), check_vma=False
    )
```

profile of v0, /device:TPU:7, one launch (start us, length us, event | category | flops | bytes accessed | tf_op | source)
XLA Modules:
  0.0 612.1 jit_solution(14909506929991602423)
XLA Ops:
  7.8 2.4 reduce-window.6
  13.2 2.0 copy.123
  16.3 1.9 select_add_fusion
  20.0 157.9 %custom-call.4 = f32[4,2,2,128,128]{3,4,2,1,0:T(8,128)} custom-call(f32[4,2,2,128,128]{4,3,2,1,0:T(8,128)S(1)} %pad_maximum_fusion), custom_call_target="InvertDiagBlocksLowerTriangular" | custom-call | tf_op jit(solution)/shard_map/jit(_solve_triangular)/vmap(vmap())/triangular_solve | solution.py:70
  190.3 2.1 convolution_bitcast_fusion
  192.5 2.1 fusion.19
  196.5 335.2 %while.39 = (s32[]{:T(128)}, f32[4,128,128]{2,1,0:T(8,128)}, f32[4,128,128]{2,1,0:T(8,128)S(1)}, f32[4,128,128]{2,1,0:T(8,128)S(1)}, f32[4,128,128]{2,1,0:T(8,128)S(1)}, /*index=5*/s32[]{:T(128)}) while((s32[]{:T(128)}, f32[4,128,128]{2,1,0:T(8,128)}, f32[4,128,128]{2,1,0:T(8,128)S(1)}, f32[4,128,128]{2,1,0:T(8,128)S(1)}, ...), condition=%wide.region_6.7_spmd, body=%wide.region_5.6_spmd.sunk | while | flops 100728832 | bytes 3145865 | solution.py:116
  196.5 3.7 collective-permute-start
  200.2 10.2 %collective-permute-done = f32[4,128,128]{2,1,0:T(8,128)S(1)} collective-permute-done((f32[4,128,128]{2,1,0:T(8,128)S(1)}, f32[4,128,128]{2,1,0:T(8,128)S(1)}, u32[]{:S(2)}, u32[]{:S(2)}) %collective-permute-start) | collective-permute-done | bytes 262176 | tf_op jit(solution)/shard_map/while/body/eval_jaxpr/ppermute | solution.py:15
  211.1 1.9 collective-permute-start
  213.0 8.6 %collective-permute-done = f32[4,128,128]{2,1,0:T(8,128)S(1)} collective-permute-done((f32[4,128,128]{2,1,0:T(8,128)S(1)}, f32[4,128,128]{2,1,0:T(8,128)S(1)}, u32[]{:S(2)}, u32[]{:S(2)}) %collective-permute-start) | collective-permute-done | bytes 262176 | tf_op jit(solution)/shard_map/while/body/eval_jaxpr/ppermute | solution.py:15
  222.4 1.9 collective-permute-start
  224.3 7.7 %collective-permute-done = f32[4,128,128]{2,1,0:T(8,128)S(1)} collective-permute-done((f32[4,128,128]{2,1,0:T(8,128)S(1)}, f32[4,128,128]{2,1,0:T(8,128)S(1)}, u32[]{:S(2)}, u32[]{:S(2)}) %collective-permute-start) | collective-permute-done | bytes 262176 | tf_op jit(solution)/shard_map/while/body/eval_jaxpr/ppermute | solution.py:15
  232.7 1.9 collective-permute-start
  234.7 7.3 %collective-permute-done = f32[4,128,128]{2,1,0:T(8,128)S(1)} collective-permute-done((f32[4,128,128]{2,1,0:T(8,128)S(1)}, f32[4,128,128]{2,1,0:T(8,128)S(1)}, u32[]{:S(2)}, u32[]{:S(2)}) %collective-permute-start) | collective-permute-done | bytes 262176 | tf_op jit(solution)/shard_map/while/body/eval_jaxpr/ppermute | solution.py:15
  242.7 1.9 collective-permute-start
  244.6 7.3 %collective-permute-done = f32[4,128,128]{2,1,0:T(8,128)S(1)} collective-permute-done((f32[4,128,128]{2,1,0:T(8,128)S(1)}, f32[4,128,128]{2,1,0:T(8,128)S(1)}, u32[]{:S(2)}, u32[]{:S(2)}) %collective-permute-start) | collective-permute-done | bytes 262176 | tf_op jit(solution)/shard_map/while/body/eval_jaxpr/ppermute | solution.py:15
  252.6 1.9 collective-permute-start
  254.5 7.3 %collective-permute-done = f32[4,128,128]{2,1,0:T(8,128)S(1)} collective-permute-done((f32[4,128,128]{2,1,0:T(8,128)S(1)}, f32[4,128,128]{2,1,0:T(8,128)S(1)}, u32[]{:S(2)}, u32[]{:S(2)}) %collective-permute-start) | collective-permute-done | bytes 262176 | tf_op jit(solution)/shard_map/while/body/eval_jaxpr/ppermute | solution.py:15
  262.6 1.9 collective-permute-start
  264.5 7.3 %collective-permute-done = f32[4,128,128]{2,1,0:T(8,128)S(1)} collective-permute-done((f32[4,128,128]{2,1,0:T(8,128)S(1)}, f32[4,128,128]{2,1,0:T(8,128)S(1)}, u32[]{:S(2)}, u32[]{:S(2)}) %collective-permute-start) | collective-permute-done | bytes 262176 | tf_op jit(solution)/shard_map/while/body/eval_jaxpr/ppermute | solution.py:15
  272.5 1.9 collective-permute-start
  274.4 7.3 %collective-permute-done = f32[4,128,128]{2,1,0:T(8,128)S(1)} collective-permute-done((f32[4,128,128]{2,1,0:T(8,128)S(1)}, f32[4,128,128]{2,1,0:T(8,128)S(1)}, u32[]{:S(2)}, u32[]{:S(2)}) %collective-permute-start) | collective-permute-done | bytes 262176 | tf_op jit(solution)/shard_map/while/body/eval_jaxpr/ppermute | solution.py:15
  282.4 1.9 collective-permute-start
  284.3 8.3 %collective-permute-done = f32[4,128,128]{2,1,0:T(8,128)S(1)} collective-permute-done((f32[4,128,128]{2,1,0:T(8,128)S(1)}, f32[4,128,128]{2,1,0:T(8,128)S(1)}, u32[]{:S(2)}, u32[]{:S(2)}) %collective-permute-start) | collective-permute-done | bytes 262176 | tf_op jit(solution)/shard_map/while/body/eval_jaxpr/ppermute | solution.py:15
  293.4 1.9 collective-permute-start
  295.3 9.4 %collective-permute-done = f32[4,128,128]{2,1,0:T(8,128)S(1)} collective-permute-done((f32[4,128,128]{2,1,0:T(8,128)S(1)}, f32[4,128,128]{2,1,0:T(8,128)S(1)}, u32[]{:S(2)}, u32[]{:S(2)}) %collective-permute-start) | collective-permute-done | bytes 262176 | tf_op jit(solution)/shard_map/while/body/eval_jaxpr/ppermute | solution.py:15
  305.4 1.9 collective-permute-start
  307.3 10.0 %collective-permute-done = f32[4,128,128]{2,1,0:T(8,128)S(1)} collective-permute-done((f32[4,128,128]{2,1,0:T(8,128)S(1)}, f32[4,128,128]{2,1,0:T(8,128)S(1)}, u32[]{:S(2)}, u32[]{:S(2)}) %collective-permute-start) | collective-permute-done | bytes 262176 | tf_op jit(solution)/shard_map/while/body/eval_jaxpr/ppermute | solution.py:15
  318.0 1.9 collective-permute-start
  319.9 9.1 %collective-permute-done = f32[4,128,128]{2,1,0:T(8,128)S(1)} collective-permute-done((f32[4,128,128]{2,1,0:T(8,128)S(1)}, f32[4,128,128]{2,1,0:T(8,128)S(1)}, u32[]{:S(2)}, u32[]{:S(2)}) %collective-permute-start) | collective-permute-done | bytes 262176 | tf_op jit(solution)/shard_map/while/body/eval_jaxpr/ppermute | solution.py:15
  329.8 1.9 collective-permute-start
  331.7 8.2 %collective-permute-done = f32[4,128,128]{2,1,0:T(8,128)S(1)} collective-permute-done((f32[4,128,128]{2,1,0:T(8,128)S(1)}, f32[4,128,128]{2,1,0:T(8,128)S(1)}, u32[]{:S(2)}, u32[]{:S(2)}) %collective-permute-start) | collective-permute-done | bytes 262176 | tf_op jit(solution)/shard_map/while/body/eval_jaxpr/ppermute | solution.py:15
  340.6 1.9 collective-permute-start
  342.5 7.3 %collective-permute-done = f32[4,128,128]{2,1,0:T(8,128)S(1)} collective-permute-done((f32[4,128,128]{2,1,0:T(8,128)S(1)}, f32[4,128,128]{2,1,0:T(8,128)S(1)}, u32[]{:S(2)}, u32[]{:S(2)}) %collective-permute-start) | collective-permute-done | bytes 262176 | tf_op jit(solution)/shard_map/while/body/eval_jaxpr/ppermute | solution.py:15
  350.5 1.9 collective-permute-start
  352.5 7.3 %collective-permute-done = f32[4,128,128]{2,1,0:T(8,128)S(1)} collective-permute-done((f32[4,128,128]{2,1,0:T(8,128)S(1)}, f32[4,128,128]{2,1,0:T(8,128)S(1)}, u32[]{:S(2)}, u32[]{:S(2)}) %collective-permute-start) | collective-permute-done | bytes 262176 | tf_op jit(solution)/shard_map/while/body/eval_jaxpr/ppermute | solution.py:15
  360.5 1.9 collective-permute-start
  362.4 7.3 %collective-permute-done = f32[4,128,128]{2,1,0:T(8,128)S(1)} collective-permute-done((f32[4,128,128]{2,1,0:T(8,128)S(1)}, f32[4,128,128]{2,1,0:T(8,128)S(1)}, u32[]{:S(2)}, u32[]{:S(2)}) %collective-permute-start) | collective-permute-done | bytes 262176 | tf_op jit(solution)/shard_map/while/body/eval_jaxpr/ppermute | solution.py:15
  370.4 1.9 collective-permute-start
  372.3 7.3 %collective-permute-done = f32[4,128,128]{2,1,0:T(8,128)S(1)} collective-permute-done((f32[4,128,128]{2,1,0:T(8,128)S(1)}, f32[4,128,128]{2,1,0:T(8,128)S(1)}, u32[]{:S(2)}, u32[]{:S(2)}) %collective-permute-start) | collective-permute-done | bytes 262176 | tf_op jit(solution)/shard_map/while/body/eval_jaxpr/ppermute | solution.py:15
  380.3 1.9 collective-permute-start
  382.3 7.3 %collective-permute-done = f32[4,128,128]{2,1,0:T(8,128)S(1)} collective-permute-done((f32[4,128,128]{2,1,0:T(8,128)S(1)}, f32[4,128,128]{2,1,0:T(8,128)S(1)}, u32[]{:S(2)}, u32[]{:S(2)}) %collective-permute-start) | collective-permute-done | bytes 262176 | tf_op jit(solution)/shard_map/while/body/eval_jaxpr/ppermute | solution.py:15
  390.3 1.9 collective-permute-start
  392.2 7.8 %collective-permute-done = f32[4,128,128]{2,1,0:T(8,128)S(1)} collective-permute-done((f32[4,128,128]{2,1,0:T(8,128)S(1)}, f32[4,128,128]{2,1,0:T(8,128)S(1)}, u32[]{:S(2)}, u32[]{:S(2)}) %collective-permute-start) | collective-permute-done | bytes 262176 | tf_op jit(solution)/shard_map/while/body/eval_jaxpr/ppermute | solution.py:15
  400.7 1.9 collective-permute-start
  402.7 8.9 %collective-permute-done = f32[4,128,128]{2,1,0:T(8,128)S(1)} collective-permute-done((f32[4,128,128]{2,1,0:T(8,128)S(1)}, f32[4,128,128]{2,1,0:T(8,128)S(1)}, u32[]{:S(2)}, u32[]{:S(2)}) %collective-permute-start) | collective-permute-done | bytes 262176 | tf_op jit(solution)/shard_map/while/body/eval_jaxpr/ppermute | solution.py:15
  412.3 1.9 collective-permute-start
  414.2 10.3 %collective-permute-done = f32[4,128,128]{2,1,0:T(8,128)S(1)} collective-permute-done((f32[4,128,128]{2,1,0:T(8,128)S(1)}, f32[4,128,128]{2,1,0:T(8,128)S(1)}, u32[]{:S(2)}, u32[]{:S(2)}) %collective-permute-start) | collective-permute-done | bytes 262176 | tf_op jit(solution)/shard_map/while/body/eval_jaxpr/ppermute | solution.py:15
  425.2 1.9 collective-permute-start
  427.1 9.6 %collective-permute-done = f32[4,128,128]{2,1,0:T(8,128)S(1)} collective-permute-done((f32[4,128,128]{2,1,0:T(8,128)S(1)}, f32[4,128,128]{2,1,0:T(8,128)S(1)}, u32[]{:S(2)}, u32[]{:S(2)}) %collective-permute-start) | collective-permute-done | bytes 262176 | tf_op jit(solution)/shard_map/while/body/eval_jaxpr/ppermute | solution.py:15
  437.4 1.9 collective-permute-start
  439.3 8.6 %collective-permute-done = f32[4,128,128]{2,1,0:T(8,128)S(1)} collective-permute-done((f32[4,128,128]{2,1,0:T(8,128)S(1)}, f32[4,128,128]{2,1,0:T(8,128)S(1)}, u32[]{:S(2)}, u32[]{:S(2)}) %collective-permute-start) | collective-permute-done | bytes 262176 | tf_op jit(solution)/shard_map/while/body/eval_jaxpr/ppermute | solution.py:15
  450.6 7.7 %collective-permute-done = f32[4,128,128]{2,1,0:T(8,128)S(1)} collective-permute-done((f32[4,128,128]{2,1,0:T(8,128)S(1)}, f32[4,128,128]{2,1,0:T(8,128)S(1)}, u32[]{:S(2)}, u32[]{:S(2)}) %collective-permute-start) | collective-permute-done | bytes 262176 | tf_op jit(solution)/shard_map/while/body/eval_jaxpr/ppermute | solution.py:15
  460.9 7.3 %collective-permute-done = f32[4,128,128]{2,1,0:T(8,128)S(1)} collective-permute-done((f32[4,128,128]{2,1,0:T(8,128)S(1)}, f32[4,128,128]{2,1,0:T(8,128)S(1)}, u32[]{:S(2)}, u32[]{:S(2)}) %collective-permute-start) | collective-permute-done | bytes 262176 | tf_op jit(solution)/shard_map/while/body/eval_jaxpr/ppermute | solution.py:15
  470.9 7.3 %collective-permute-done = f32[4,128,128]{2,1,0:T(8,128)S(1)} collective-permute-done((f32[4,128,128]{2,1,0:T(8,128)S(1)}, f32[4,128,128]{2,1,0:T(8,128)S(1)}, u32[]{:S(2)}, u32[]{:S(2)}) %collective-permute-start) | collective-permute-done | bytes 262176 | tf_op jit(solution)/shard_map/while/body/eval_jaxpr/ppermute | solution.py:15
  480.8 7.3 %collective-permute-done = f32[4,128,128]{2,1,0:T(8,128)S(1)} collective-permute-done((f32[4,128,128]{2,1,0:T(8,128)S(1)}, f32[4,128,128]{2,1,0:T(8,128)S(1)}, u32[]{:S(2)}, u32[]{:S(2)}) %collective-permute-start) | collective-permute-done | bytes 262176 | tf_op jit(solution)/shard_map/while/body/eval_jaxpr/ppermute | solution.py:15
  490.8 7.3 %collective-permute-done = f32[4,128,128]{2,1,0:T(8,128)S(1)} collective-permute-done((f32[4,128,128]{2,1,0:T(8,128)S(1)}, f32[4,128,128]{2,1,0:T(8,128)S(1)}, u32[]{:S(2)}, u32[]{:S(2)}) %collective-permute-start) | collective-permute-done | bytes 262176 | tf_op jit(solution)/shard_map/while/body/eval_jaxpr/ppermute | solution.py:15
  500.7 7.3 %collective-permute-done = f32[4,128,128]{2,1,0:T(8,128)S(1)} collective-permute-done((f32[4,128,128]{2,1,0:T(8,128)S(1)}, f32[4,128,128]{2,1,0:T(8,128)S(1)}, u32[]{:S(2)}, u32[]{:S(2)}) %collective-permute-start) | collective-permute-done | bytes 262176 | tf_op jit(solution)/shard_map/while/body/eval_jaxpr/ppermute | solution.py:15
  510.6 8.3 %collective-permute-done = f32[4,128,128]{2,1,0:T(8,128)S(1)} collective-permute-done((f32[4,128,128]{2,1,0:T(8,128)S(1)}, f32[4,128,128]{2,1,0:T(8,128)S(1)}, u32[]{:S(2)}, u32[]{:S(2)}) %collective-permute-start) | collective-permute-done | bytes 262176 | tf_op jit(solution)/shard_map/while/body/eval_jaxpr/ppermute | solution.py:15
  521.6 9.4 %collective-permute-done = f32[4,128,128]{2,1,0:T(8,128)S(1)} collective-permute-done((f32[4,128,128]{2,1,0:T(8,128)S(1)}, f32[4,128,128]{2,1,0:T(8,128)S(1)}, u32[]{:S(2)}, u32[]{:S(2)}) %collective-permute-start) | collective-permute-done | bytes 262176 | tf_op jit(solution)/shard_map/while/body/eval_jaxpr/ppermute | solution.py:15
  531.7 4.9 while.40
  537.3 4.3 fusion.45
  541.6 62.0 %reduce-scatter.2.cloned.1.call-done = f32[16,4096]{1,0:T(8,128)} async-done(((f32[128,4096]{1,0:T(8,128)}), f32[16,4096]{1,0:T(8,128)}) %reduce-scatter.2.cloned.1.call-update) | async-done | bytes 262160 | tf_op jit(solution)/shard_map/reduce_scatter | solution.py:138
  (207 shorter events, 67.3 us)
Async XLA Ops:
  6.5 530.5 %copy-start = (f32[128]{0:T(128)S(1)}, f32[128]{0:T(128)}, u32[]{:S(2)}) copy-start(f32[128]{0:T(128)} %param.20) | copy-start | bytes 1540
  6.5 4.3 copy-start.11
  6.5 597.1 %reduce-scatter.2.cloned.1.call-start = ((), (), s32[]{:S(2)}) async-start(), calls=%async_computation.1 | async-start | bytes 2359296 | tf_op jit(solution)/shard_map/reduce_scatter | solution.py:138
  7.5 4.9 copy-start.7
  12.4 3.9 copy-start.9
  18.2 1.4 copy-start.5
  179.9 1.2 copy-start.6
  183.9 2.6 copy-start.12
  183.9 2.7 copy-start.10
  188.5 1.7 copy-start.4
  196.4 335.2 %copy-start.2 = (f32[2,4,64,128]{3,2,0,1:T(8,128)S(1)}, f32[2,4,64,128]{3,2,0,1:T(8,128)}, u32[]{:S(2)}) copy-start(f32[2,4,64,128]{3,2,0,1:T(8,128)} %fusion.21) | copy-start | bytes 786436
  196.5 335.2 %copy-start.3 = (f32[2,4,64,128]{3,2,1,0:T(8,128)S(1)}, f32[2,4,64,128]{3,2,1,0:T(8,128)}, u32[]{:S(2)}) copy-start(f32[2,4,64,128]{3,2,1,0:T(8,128)} %custom-call.7) | copy-start | bytes 786436
  196.5 13.9 %collective-permute-start = (f32[4,128,128]{2,1,0:T(8,128)S(1)}, f32[4,128,128]{2,1,0:T(8,128)S(1)}, u32[]{:S(2)}, u32[]{:S(2)}) collective-permute-start(f32[4,128,128]{2,1,0:T(8,128)S(1)} %get-tuple-element.377), channel_id=1, source_target_pairs={{0,8},{8,16},{16,24},{24,32},{32,40},{40,48},{48,56},{56,64},{64,7... | collective-permute-start | bytes 786440 | tf_op jit(solution)/shard_map/while/body/eval_jaxpr/ppermute | solution.py:15
  210.4 0.7 copy-start.1
  211.1 10.6 %collective-permute-start = (f32[4,128,128]{2,1,0:T(8,128)S(1)}, f32[4,128,128]{2,1,0:T(8,128)S(1)}, u32[]{:S(2)}, u32[]{:S(2)}) collective-permute-start(f32[4,128,128]{2,1,0:T(8,128)S(1)} %get-tuple-element.377), channel_id=1, source_target_pairs={{0,8},{8,16},{16,24},{24,32},{32,40},{40,48},{48,56},{56,64},{64,7... | collective-permute-start | bytes 786440 | tf_op jit(solution)/shard_map/while/body/eval_jaxpr/ppermute | solution.py:15
  221.7 0.7 copy-start.1
  222.4 9.6 %collective-permute-start = (f32[4,128,128]{2,1,0:T(8,128)S(1)}, f32[4,128,128]{2,1,0:T(8,128)S(1)}, u32[]{:S(2)}, u32[]{:S(2)}) collective-permute-start(f32[4,128,128]{2,1,0:T(8,128)S(1)} %get-tuple-element.377), channel_id=1, source_target_pairs={{0,8},{8,16},{16,24},{24,32},{32,40},{40,48},{48,56},{56,64},{64,7... | collective-permute-start | bytes 786440 | tf_op jit(solution)/shard_map/while/body/eval_jaxpr/ppermute | solution.py:15
  232.0 0.7 copy-start.1
  232.7 9.2 %collective-permute-start = (f32[4,128,128]{2,1,0:T(8,128)S(1)}, f32[4,128,128]{2,1,0:T(8,128)S(1)}, u32[]{:S(2)}, u32[]{:S(2)}) collective-permute-start(f32[4,128,128]{2,1,0:T(8,128)S(1)} %get-tuple-element.377), channel_id=1, source_target_pairs={{0,8},{8,16},{16,24},{24,32},{32,40},{40,48},{48,56},{56,64},{64,7... | collective-permute-start | bytes 786440 | tf_op jit(solution)/shard_map/while/body/eval_jaxpr/ppermute | solution.py:15
  242.7 9.2 %collective-permute-start = (f32[4,128,128]{2,1,0:T(8,128)S(1)}, f32[4,128,128]{2,1,0:T(8,128)S(1)}, u32[]{:S(2)}, u32[]{:S(2)}) collective-permute-start(f32[4,128,128]{2,1,0:T(8,128)S(1)} %get-tuple-element.377), channel_id=1, source_target_pairs={{0,8},{8,16},{16,24},{24,32},{32,40},{40,48},{48,56},{56,64},{64,7... | collective-permute-start | bytes 786440 | tf_op jit(solution)/shard_map/while/body/eval_jaxpr/ppermute | solution.py:15
  251.9 0.7 copy-start.1
  252.6 9.2 %collective-permute-start = (f32[4,128,128]{2,1,0:T(8,128)S(1)}, f32[4,128,128]{2,1,0:T(8,128)S(1)}, u32[]{:S(2)}, u32[]{:S(2)}) collective-permute-start(f32[4,128,128]{2,1,0:T(8,128)S(1)} %get-tuple-element.377), channel_id=1, source_target_pairs={{0,8},{8,16},{16,24},{24,32},{32,40},{40,48},{48,56},{56,64},{64,7... | collective-permute-start | bytes 786440 | tf_op jit(solution)/shard_map/while/body/eval_jaxpr/ppermute | solution.py:15
  262.6 9.2 %collective-permute-start = (f32[4,128,128]{2,1,0:T(8,128)S(1)}, f32[4,128,128]{2,1,0:T(8,128)S(1)}, u32[]{:S(2)}, u32[]{:S(2)}) collective-permute-start(f32[4,128,128]{2,1,0:T(8,128)S(1)} %get-tuple-element.377), channel_id=1, source_target_pairs={{0,8},{8,16},{16,24},{24,32},{32,40},{40,48},{48,56},{56,64},{64,7... | collective-permute-start | bytes 786440 | tf_op jit(solution)/shard_map/while/body/eval_jaxpr/ppermute | solution.py:15
  271.8 0.7 copy-start.1
  272.5 9.2 %collective-permute-start = (f32[4,128,128]{2,1,0:T(8,128)S(1)}, f32[4,128,128]{2,1,0:T(8,128)S(1)}, u32[]{:S(2)}, u32[]{:S(2)}) collective-permute-start(f32[4,128,128]{2,1,0:T(8,128)S(1)} %get-tuple-element.377), channel_id=1, source_target_pairs={{0,8},{8,16},{16,24},{24,32},{32,40},{40,48},{48,56},{56,64},{64,7... | collective-permute-start | bytes 786440 | tf_op jit(solution)/shard_map/while/body/eval_jaxpr/ppermute | solution.py:15
  281.7 0.7 copy-start.1
  282.4 10.2 %collective-permute-start = (f32[4,128,128]{2,1,0:T(8,128)S(1)}, f32[4,128,128]{2,1,0:T(8,128)S(1)}, u32[]{:S(2)}, u32[]{:S(2)}) collective-permute-start(f32[4,128,128]{2,1,0:T(8,128)S(1)} %get-tuple-element.377), channel_id=1, source_target_pairs={{0,8},{8,16},{16,24},{24,32},{32,40},{40,48},{48,56},{56,64},{64,7... | collective-permute-start | bytes 786440 | tf_op jit(solution)/shard_map/while/body/eval_jaxpr/ppermute | solution.py:15
  292.6 0.7 copy-start.1
  293.4 11.3 %collective-permute-start = (f32[4,128,128]{2,1,0:T(8,128)S(1)}, f32[4,128,128]{2,1,0:T(8,128)S(1)}, u32[]{:S(2)}, u32[]{:S(2)}) collective-permute-start(f32[4,128,128]{2,1,0:T(8,128)S(1)} %get-tuple-element.377), channel_id=1, source_target_pairs={{0,8},{8,16},{16,24},{24,32},{32,40},{40,48},{48,56},{56,64},{64,7... | collective-permute-start | bytes 786440 | tf_op jit(solution)/shard_map/while/body/eval_jaxpr/ppermute | solution.py:15
  304.7 0.7 copy-start.1
  305.4 11.9 %collective-permute-start = (f32[4,128,128]{2,1,0:T(8,128)S(1)}, f32[4,128,128]{2,1,0:T(8,128)S(1)}, u32[]{:S(2)}, u32[]{:S(2)}) collective-permute-start(f32[4,128,128]{2,1,0:T(8,128)S(1)} %get-tuple-element.377), channel_id=1, source_target_pairs={{0,8},{8,16},{16,24},{24,32},{32,40},{40,48},{48,56},{56,64},{64,7... | collective-permute-start | bytes 786440 | tf_op jit(solution)/shard_map/while/body/eval_jaxpr/ppermute | solution.py:15
  317.3 0.7 copy-start.1
  318.0 11.0 %collective-permute-start = (f32[4,128,128]{2,1,0:T(8,128)S(1)}, f32[4,128,128]{2,1,0:T(8,128)S(1)}, u32[]{:S(2)}, u32[]{:S(2)}) collective-permute-start(f32[4,128,128]{2,1,0:T(8,128)S(1)} %get-tuple-element.377), channel_id=1, source_target_pairs={{0,8},{8,16},{16,24},{24,32},{32,40},{40,48},{48,56},{56,64},{64,7... | collective-permute-start | bytes 786440 | tf_op jit(solution)/shard_map/while/body/eval_jaxpr/ppermute | solution.py:15
  329.1 0.7 copy-start.1
  329.8 10.1 %collective-permute-start = (f32[4,128,128]{2,1,0:T(8,128)S(1)}, f32[4,128,128]{2,1,0:T(8,128)S(1)}, u32[]{:S(2)}, u32[]{:S(2)}) collective-permute-start(f32[4,128,128]{2,1,0:T(8,128)S(1)} %get-tuple-element.377), channel_id=1, source_target_pairs={{0,8},{8,16},{16,24},{24,32},{32,40},{40,48},{48,56},{56,64},{64,7... | collective-permute-start | bytes 786440 | tf_op jit(solution)/shard_map/while/body/eval_jaxpr/ppermute | solution.py:15
  339.9 0.7 copy-start.1
  340.6 9.2 %collective-permute-start = (f32[4,128,128]{2,1,0:T(8,128)S(1)}, f32[4,128,128]{2,1,0:T(8,128)S(1)}, u32[]{:S(2)}, u32[]{:S(2)}) collective-permute-start(f32[4,128,128]{2,1,0:T(8,128)S(1)} %get-tuple-element.377), channel_id=1, source_target_pairs={{0,8},{8,16},{16,24},{24,32},{32,40},{40,48},{48,56},{56,64},{64,7... | collective-permute-start | bytes 786440 | tf_op jit(solution)/shard_map/while/body/eval_jaxpr/ppermute | solution.py:15
  349.8 0.7 copy-start.1
  350.5 9.2 %collective-permute-start = (f32[4,128,128]{2,1,0:T(8,128)S(1)}, f32[4,128,128]{2,1,0:T(8,128)S(1)}, u32[]{:S(2)}, u32[]{:S(2)}) collective-permute-start(f32[4,128,128]{2,1,0:T(8,128)S(1)} %get-tuple-element.377), channel_id=1, source_target_pairs={{0,8},{8,16},{16,24},{24,32},{32,40},{40,48},{48,56},{56,64},{64,7... | collective-permute-start | bytes 786440 | tf_op jit(solution)/shard_map/while/body/eval_jaxpr/ppermute | solution.py:15
  360.5 9.2 %collective-permute-start = (f32[4,128,128]{2,1,0:T(8,128)S(1)}, f32[4,128,128]{2,1,0:T(8,128)S(1)}, u32[]{:S(2)}, u32[]{:S(2)}) collective-permute-start(f32[4,128,128]{2,1,0:T(8,128)S(1)} %get-tuple-element.377), channel_id=1, source_target_pairs={{0,8},{8,16},{16,24},{24,32},{32,40},{40,48},{48,56},{56,64},{64,7... | collective-permute-start | bytes 786440 | tf_op jit(solution)/shard_map/while/body/eval_jaxpr/ppermute | solution.py:15
  369.7 0.7 copy-start.1
  370.4 9.2 %collective-permute-start = (f32[4,128,128]{2,1,0:T(8,128)S(1)}, f32[4,128,128]{2,1,0:T(8,128)S(1)}, u32[]{:S(2)}, u32[]{:S(2)}) collective-permute-start(f32[4,128,128]{2,1,0:T(8,128)S(1)} %get-tuple-element.377), channel_id=1, source_target_pairs={{0,8},{8,16},{16,24},{24,32},{32,40},{40,48},{48,56},{56,64},{64,7... | collective-permute-start | bytes 786440 | tf_op jit(solution)/shard_map/while/body/eval_jaxpr/ppermute | solution.py:15
  380.3 9.2 %collective-permute-start = (f32[4,128,128]{2,1,0:T(8,128)S(1)}, f32[4,128,128]{2,1,0:T(8,128)S(1)}, u32[]{:S(2)}, u32[]{:S(2)}) collective-permute-start(f32[4,128,128]{2,1,0:T(8,128)S(1)} %get-tuple-element.377), channel_id=1, source_target_pairs={{0,8},{8,16},{16,24},{24,32},{32,40},{40,48},{48,56},{56,64},{64,7... | collective-permute-start | bytes 786440 | tf_op jit(solution)/shard_map/while/body/eval_jaxpr/ppermute | solution.py:15
  389.6 0.7 copy-start.1
  390.3 9.7 %collective-permute-start = (f32[4,128,128]{2,1,0:T(8,128)S(1)}, f32[4,128,128]{2,1,0:T(8,128)S(1)}, u32[]{:S(2)}, u32[]{:S(2)}) collective-permute-start(f32[4,128,128]{2,1,0:T(8,128)S(1)} %get-tuple-element.377), channel_id=1, source_target_pairs={{0,8},{8,16},{16,24},{24,32},{32,40},{40,48},{48,56},{56,64},{64,7... | collective-permute-start | bytes 786440 | tf_op jit(solution)/shard_map/while/body/eval_jaxpr/ppermute | solution.py:15
  400.0 0.7 copy-start.1
  400.7 10.8 %collective-permute-start = (f32[4,128,128]{2,1,0:T(8,128)S(1)}, f32[4,128,128]{2,1,0:T(8,128)S(1)}, u32[]{:S(2)}, u32[]{:S(2)}) collective-permute-start(f32[4,128,128]{2,1,0:T(8,128)S(1)} %get-tuple-element.377), channel_id=1, source_target_pairs={{0,8},{8,16},{16,24},{24,32},{32,40},{40,48},{48,56},{56,64},{64,7... | collective-permute-start | bytes 786440 | tf_op jit(solution)/shard_map/while/body/eval_jaxpr/ppermute | solution.py:15
  411.6 0.7 copy-start.1
  412.3 12.2 %collective-permute-start = (f32[4,128,128]{2,1,0:T(8,128)S(1)}, f32[4,128,128]{2,1,0:T(8,128)S(1)}, u32[]{:S(2)}, u32[]{:S(2)}) collective-permute-start(f32[4,128,128]{2,1,0:T(8,128)S(1)} %get-tuple-element.377), channel_id=1, source_target_pairs={{0,8},{8,16},{16,24},{24,32},{32,40},{40,48},{48,56},{56,64},{64,7... | collective-permute-start | bytes 786440 | tf_op jit(solution)/shard_map/while/body/eval_jaxpr/ppermute | solution.py:15
  425.2 11.5 %collective-permute-start = (f32[4,128,128]{2,1,0:T(8,128)S(1)}, f32[4,128,128]{2,1,0:T(8,128)S(1)}, u32[]{:S(2)}, u32[]{:S(2)}) collective-permute-start(f32[4,128,128]{2,1,0:T(8,128)S(1)} %get-tuple-element.377), channel_id=1, source_target_pairs={{0,8},{8,16},{16,24},{24,32},{32,40},{40,48},{48,56},{56,64},{64,7... | collective-permute-start | bytes 786440 | tf_op jit(solution)/shard_map/while/body/eval_jaxpr/ppermute | solution.py:15
  436.7 0.7 copy-start.1
  437.4 10.6 %collective-permute-start = (f32[4,128,128]{2,1,0:T(8,128)S(1)}, f32[4,128,128]{2,1,0:T(8,128)S(1)}, u32[]{:S(2)}, u32[]{:S(2)}) collective-permute-start(f32[4,128,128]{2,1,0:T(8,128)S(1)} %get-tuple-element.377), channel_id=1, source_target_pairs={{0,8},{8,16},{16,24},{24,32},{32,40},{40,48},{48,56},{56,64},{64,7... | collective-permute-start | bytes 786440 | tf_op jit(solution)/shard_map/while/body/eval_jaxpr/ppermute | solution.py:15
  448.7 9.6 %collective-permute-start = (f32[4,128,128]{2,1,0:T(8,128)S(1)}, f32[4,128,128]{2,1,0:T(8,128)S(1)}, u32[]{:S(2)}, u32[]{:S(2)}) collective-permute-start(f32[4,128,128]{2,1,0:T(8,128)S(1)} %get-tuple-element.377), channel_id=1, source_target_pairs={{0,8},{8,16},{16,24},{24,32},{32,40},{40,48},{48,56},{56,64},{64,7... | collective-permute-start | bytes 786440 | tf_op jit(solution)/shard_map/while/body/eval_jaxpr/ppermute | solution.py:15
  458.3 0.7 copy-start.1
  459.0 9.2 %collective-permute-start = (f32[4,128,128]{2,1,0:T(8,128)S(1)}, f32[4,128,128]{2,1,0:T(8,128)S(1)}, u32[]{:S(2)}, u32[]{:S(2)}) collective-permute-start(f32[4,128,128]{2,1,0:T(8,128)S(1)} %get-tuple-element.377), channel_id=1, source_target_pairs={{0,8},{8,16},{16,24},{24,32},{32,40},{40,48},{48,56},{56,64},{64,7... | collective-permute-start | bytes 786440 | tf_op jit(solution)/shard_map/while/body/eval_jaxpr/ppermute | solution.py:15
  469.0 9.2 %collective-permute-start = (f32[4,128,128]{2,1,0:T(8,128)S(1)}, f32[4,128,128]{2,1,0:T(8,128)S(1)}, u32[]{:S(2)}, u32[]{:S(2)}) collective-permute-start(f32[4,128,128]{2,1,0:T(8,128)S(1)} %get-tuple-element.377), channel_id=1, source_target_pairs={{0,8},{8,16},{16,24},{24,32},{32,40},{40,48},{48,56},{56,64},{64,7... | collective-permute-start | bytes 786440 | tf_op jit(solution)/shard_map/while/body/eval_jaxpr/ppermute | solution.py:15
  478.2 0.7 copy-start.1
  478.9 9.2 %collective-permute-start = (f32[4,128,128]{2,1,0:T(8,128)S(1)}, f32[4,128,128]{2,1,0:T(8,128)S(1)}, u32[]{:S(2)}, u32[]{:S(2)}) collective-permute-start(f32[4,128,128]{2,1,0:T(8,128)S(1)} %get-tuple-element.377), channel_id=1, source_target_pairs={{0,8},{8,16},{16,24},{24,32},{32,40},{40,48},{48,56},{56,64},{64,7... | collective-permute-start | bytes 786440 | tf_op jit(solution)/shard_map/while/body/eval_jaxpr/ppermute | solution.py:15
  488.8 9.2 %collective-permute-start = (f32[4,128,128]{2,1,0:T(8,128)S(1)}, f32[4,128,128]{2,1,0:T(8,128)S(1)}, u32[]{:S(2)}, u32[]{:S(2)}) collective-permute-start(f32[4,128,128]{2,1,0:T(8,128)S(1)} %get-tuple-element.377), channel_id=1, source_target_pairs={{0,8},{8,16},{16,24},{24,32},{32,40},{40,48},{48,56},{56,64},{64,7... | collective-permute-start | bytes 786440 | tf_op jit(solution)/shard_map/while/body/eval_jaxpr/ppermute | solution.py:15
  498.0 0.7 copy-start.1
  498.8 9.2 %collective-permute-start = (f32[4,128,128]{2,1,0:T(8,128)S(1)}, f32[4,128,128]{2,1,0:T(8,128)S(1)}, u32[]{:S(2)}, u32[]{:S(2)}) collective-permute-start(f32[4,128,128]{2,1,0:T(8,128)S(1)} %get-tuple-element.377), channel_id=1, source_target_pairs={{0,8},{8,16},{16,24},{24,32},{32,40},{40,48},{48,56},{56,64},{64,7... | collective-permute-start | bytes 786440 | tf_op jit(solution)/shard_map/while/body/eval_jaxpr/ppermute | solution.py:15
  508.7 10.2 %collective-permute-start = (f32[4,128,128]{2,1,0:T(8,128)S(1)}, f32[4,128,128]{2,1,0:T(8,128)S(1)}, u32[]{:S(2)}, u32[]{:S(2)}) collective-permute-start(f32[4,128,128]{2,1,0:T(8,128)S(1)} %get-tuple-element.377), channel_id=1, source_target_pairs={{0,8},{8,16},{16,24},{24,32},{32,40},{40,48},{48,56},{56,64},{64,7... | collective-permute-start | bytes 786440 | tf_op jit(solution)/shard_map/while/body/eval_jaxpr/ppermute | solution.py:15
  519.6 11.3 %collective-permute-start = (f32[4,128,128]{2,1,0:T(8,128)S(1)}, f32[4,128,128]{2,1,0:T(8,128)S(1)}, u32[]{:S(2)}, u32[]{:S(2)}) collective-permute-start(f32[4,128,128]{2,1,0:T(8,128)S(1)} %get-tuple-element.377), channel_id=1, source_target_pairs={{0,8},{8,16},{16,24},{24,32},{32,40},{40,48},{48,56},{56,64},{64,7... | collective-permute-start | bytes 786440 | tf_op jit(solution)/shard_map/while/body/eval_jaxpr/ppermute | solution.py:15
  531.7 5.6 copy-start.8
  (11 other events, 7.9 us)
Sparse Core Ops, SparseCore 0:
  541.7 61.8 reduce-scatter.1
where the time goes:
time: 616 us; the launch traced here: 612 us
  waiting for transfers between devices  314 us (51%)
  other arithmetic  166 us (27%)
  starting transfers between devices  60.9 us (10%)
  matrix products  34.2 us (6%)
  local copies, waits for them, and re-layouts  22.6 us (4%)
  between operations  13.8 us (2%)
    ppermute x31, waiting for transfers between devices, shifted(): return lax.ppermute(value, axis, pairs)  252 us
    another operation x6, other arithmetic, on_device(): jax.scipy.linalg.solve_triangular(system, right_side, lower=True, unit_di...  158 us
    reduce_scatter x1, waiting for transfers between devices, on_device(): lax.psum_scatter(jnp.dot(gated, w_out, preferred_element_type=jnp.float32...  62 us
    ppermute x31, starting transfers between devices, shifted(): return lax.ppermute(value, axis, pairs)  60.9 us
    dot_general x37, matrix products, chain_product(): jnp.einsum('hde,hef->hdf', left_mat, right_mat, precision=full_precision)  16.2 us
  transfers between devices with their start and end apart: 32, of which 32 were waited for; matrix products, arithmetic and copies ran while one was open for 0% of the time, Pallas kernels for 0%

commit v1 on v0

v1 whole, which is shorter than its diff:
```python
import functools

import jax
import jax.numpy as jnp
from jax import lax
from jax.experimental import pallas as pl
from jax.experimental.pallas import tpu as pltpu
from jax.sharding import PartitionSpec as P

F32 = jnp.float32
BF16 = jnp.bfloat16
EXACT = lax.Precision.HIGHEST
W = 128
STEPS = 3
MICRO = STEPS * W
HEADS = 4
BASE = 32
LINE = 8
ROWS = 4
RING = 4
CHUNKS = 4
MESH = pl.DeviceIdType.MESH


def iota(shape, dim):
    return lax.broadcasted_iota(jnp.int32, shape, dim)


def split(a):
    hi = a.astype(BF16)
    return hi, (a - hi.astype(F32)).astype(BF16)


def lhs_of(a):
    return jnp.concatenate(split(a), axis=1)


def rhs_of(b):
    pair = jnp.concatenate(split(b), axis=1)
    return jnp.concatenate([pair, pair], axis=0)


def mm(left, right):
    out = jnp.dot(left, right, preferred_element_type=F32)
    half = out.shape[1] // 2
    return out[:, :half] + out[:, half:]


def nt(a, b, precision=None):
    return lax.dot_general(
        a, b, (((1,), (1,)), ((), ())), preferred_element_type=F32, precision=precision
    )


def local_maps(k_ref, v_ref, beta_ref, decay_ref, tf_ref, x_ref, emit):
    step_i, token_i = iota((MICRO, W), 0), iota((MICRO, W), 1)
    upto = (STEPS * token_i <= step_i).astype(F32)
    decay = jnp.maximum(decay_ref[...], -110.0)
    g_col = nt(upto, decay, EXACT)
    g_row = nt(decay, upto, EXACT)
    b_col = sum(
        nt((STEPS * token_i + j == step_i).astype(F32), beta_ref[j], EXACT) for j in range(STEPS)
    )
    row_i, col_i = iota((W, W), 0), iota((W, W), 1)
    strict = row_i > col_i
    eye = (row_i == col_i).astype(F32)
    ones = jnp.ones((8, 2 * W), BF16)
    lane_block = iota((BASE, W), 1) // BASE
    r_cols, r_rows, systems, packed = [], [], [], []
    for h in range(HEADS):
        keys = k_ref[:, h * W : (h + 1) * W]
        wide = keys.astype(F32)
        squares = wide * wide
        r_c = 1.0 / jnp.sqrt(jnp.sum(squares, axis=1, keepdims=True) + 1e-6)
        r_r = 1.0 / jnp.sqrt(nt(ones, lhs_of(squares))[0:1] + 1e-6)
        r_cols.append(r_c)
        r_rows.append(r_r)
        scale = b_col[:, h : h + 1] * r_c
        blocks = {}
        for i in range(3):
            for j in range(i + 1):
                si, sj = slice(i * W, (i + 1) * W), slice(j * W, (j + 1) * W)
                gap = g_col[si, h : h + 1] - g_row[h : h + 1, sj]
                if i == j:
                    gap = jnp.where(strict, gap, 0.0)
                a = nt(keys[si], keys[sj]) * (scale[si] * r_r[:, sj]) * jnp.exp(gap)
                if i == j:
                    a = jnp.where(strict, a, 0.0)
                    packed.append(
                        sum(
                            jnp.where(lane_block == b, a[b * BASE : (b + 1) * BASE], 0.0)
                            for b in range(W // BASE)
                        )
                    )
                blocks[i, j] = a
        systems.append(blocks)
    count = len(packed)
    packed = lhs_of(jnp.concatenate(packed, axis=0))
    block_start = (col_i // BASE) * BASE
    small = [
        (iota((count, 8, W), 1) + 8 * s == iota((count, 8, W), 2) % BASE).astype(F32)
        for s in range(BASE // 8)
    ]
    for j in range(BASE - 1):
        pick = (row_i == block_start + j).astype(BF16)
        factor = jnp.dot(
            packed, jnp.concatenate([pick, pick], axis=0), preferred_element_type=F32
        ).reshape(count, BASE, W)
        first = j // 8
        row = small[first][:, j % 8 : j % 8 + 1, :]
        for s in range(first, BASE // 8):
            small[s] = small[s] - factor[:, 8 * s : 8 * s + 8, :] * row
    same32 = (row_i // 32) == (col_i // 32)
    same64 = (row_i // 64) == (col_i // 64)
    low32 = same64 & jnp.logical_not(same32)
    low64 = jnp.logical_not(same64)
    for h in range(HEADS):
        wide = k_ref[:, h * W : (h + 1) * W].astype(F32)
        inverse = []
        for i in range(3):
            n = h * 3 + i
            tile = jnp.concatenate([small[s][n] for s in range(BASE // 8)], axis=0)
            inv = jnp.where(same32, jnp.concatenate([tile] * (W // BASE), axis=0), 0.0)
            for low in (low32, low64):
                step = mm(lhs_of(inv), rhs_of(jnp.where(low, systems[h][i, i], 0.0)))
                inv = inv - mm(lhs_of(step), rhs_of(inv))
            inverse.append(lhs_of(inv))
        b_c, g_c = b_col[:, h : h + 1], g_col[:, h : h + 1]
        right = jnp.concatenate(
            [
                b_c * v_ref[:, h * W : (h + 1) * W].astype(F32),
                (b_c * jnp.exp(g_c) * r_cols[h]) * wide,
            ],
            axis=1,
        )
        x1 = mm(inverse[0], rhs_of(right[:W]))
        x1r = rhs_of(x1)
        x2 = mm(inverse[1], rhs_of(right[W : 2 * W] - mm(lhs_of(systems[h][1, 0]), x1r)))
        x3 = mm(
            inverse[2],
            rhs_of(
                right[2 * W :]
                - mm(lhs_of(systems[h][2, 0]), x1r)
                - mm(lhs_of(systems[h][2, 1]), rhs_of(x2))
            ),
        )
        solved = jnp.concatenate([x1, x2, x3], axis=0)
        x_ref[h] = rhs_of(solved)
        g_end = g_col[MICRO - 1 : MICRO, h : h + 1]
        tail = jnp.concatenate(split((r_cols[h] * jnp.exp(g_end - g_c)) * solved), axis=1)
        out = jnp.dot(wide.T.astype(BF16), tail, preferred_element_type=F32)
        out = out[:, : 2 * W] + out[:, 2 * W :]
        tf_ref[h, 0] = jnp.exp(g_end) * eye - out[:, W:]
        tf_ref[h, 1] = out[:, :W]
        emit(h)
    return g_row, r_rows


def local_reads(q_ref, k_ref, decay_ref, x_ref, g_row, r_rows, lo_ref, lq_ref):
    decay = jnp.maximum(decay_ref[...], -110.0)
    upto = (iota((W, W), 1) <= iota((W, W), 0)).astype(F32)
    q_col = nt(upto, decay, EXACT)
    visible = iota((W, MICRO), 1) <= STEPS * iota((W, MICRO), 0) + STEPS - 1
    for h in range(HEADS):
        keys = k_ref[:, h * W : (h + 1) * W]
        query = q_ref[:, h * W : (h + 1) * W]
        gap = jnp.where(visible, q_col[:, h : h + 1] - g_row[h : h + 1, :], 0.0)
        scores = jnp.where(visible, nt(query, keys) * (r_rows[h] * jnp.exp(gap)), 0.0)
        reads = mm(lhs_of(scores), x_ref[h])
        lo_ref[h] = reads[:, :W]
        lq_ref[h] = lhs_of(jnp.exp(q_col[:, h : h + 1]) * query.astype(F32) - reads[:, W:])


def compose(lefts, right):
    out = mm(
        jnp.concatenate([lhs_of(t) for t, f in lefts], axis=0),
        rhs_of(jnp.concatenate(right, axis=1)),
    )
    return [
        (out[i * W : (i + 1) * W, :W], out[i * W : (i + 1) * W, W:] + lefts[i][1])
        for i in range(len(lefts))
    ]


def layer_kernel(
    q_ref, k_ref, v_ref, gate_ref, beta_ref, decay_ref, gain_ref, w_hbm, out_ref,
    w_ref, tf_ref, x_ref, lo_ref, lq_ref, act_ref,
    maps_ref, pre_t_ref, pre_f_ref, total_ref, far_ref, line_ref, next_ref, given_ref, start_ref,
    gated_ref, pair_out, pair_in, own_ref, relay_in, side_in,
    w_sem, map_send, map_recv, line_send, line_recv, start_send, start_recv,
    pair_send, pair_recv, ring_send, ring_recv,
):
    seq, head = lax.axis_index("seq"), lax.axis_index("head")
    x, z = seq // LINE, lax.rem(seq, LINE)
    y, core = head // 2, lax.rem(head, 2)
    line = x * LINE

    def at(s, h):
        return {"device_id": (s, h), "device_id_type": MESH}

    up = lax.rem(y + 1, RING) * 2 + core
    down = lax.rem(y + RING - 1, RING) * 2 + core
    sibling = y * 2 + 1 - core

    w_copy = pltpu.make_async_copy(w_hbm, w_ref, w_sem)
    w_copy.start()

    barrier = pltpu.get_barrier_semaphore()
    for i in range(1, LINE):
        pl.semaphore_signal(barrier, inc=1, **at(line + lax.rem(z + i, LINE), head))
    for i in range(1, ROWS):
        pl.semaphore_signal(barrier, inc=1, **at(lax.rem(x + i, ROWS) * LINE + z, head))
    for h in (up, down, sibling):
        pl.semaphore_signal(barrier, inc=1, **at(seq, h))
    pl.semaphore_wait(barrier, LINE - 1 + ROWS - 1 + 3)

    def map_copy(h):
        return pltpu.make_async_remote_copy(
            src_ref=tf_ref.at[h], dst_ref=maps_ref.at[z],
            send_sem=map_send.at[h], recv_sem=map_recv.at[z], **at(line + 2 * h, head),
        )

    def emit(h):
        @pl.when(z != 2 * h)
        def _():
            map_copy(h).start()

        @pl.when(z == 2 * h)
        def _():
            maps_ref[z] = tf_ref[h]

    g_row, r_rows = local_maps(k_ref, v_ref, beta_ref, decay_ref, tf_ref, x_ref, emit)
    local_reads(q_ref, k_ref, decay_ref, x_ref, g_row, r_rows, lo_ref, lq_ref)
    gate = gate_ref[...].astype(F32)
    act_ref[...] = (gate / (1.0 + jnp.exp(-gate))) * jnp.concatenate([gain_ref[...]] * HEADS, axis=1)

    owner = lax.rem(z, 2) == 0
    mine = z // 2

    def line_copy(src, dst, send, recv, to):
        return pltpu.make_async_remote_copy(
            src_ref=src, dst_ref=dst, send_sem=line_send.at[send], recv_sem=line_recv.at[recv],
            **at(to * LINE + z, head),
        )

    @pl.when(owner)
    def _():
        for i in range(1, LINE):
            other = lax.rem(z + i, LINE)
            pltpu.make_async_remote_copy(
                src_ref=tf_ref.at[0], dst_ref=maps_ref.at[other],
                send_sem=map_send.at[0], recv_sem=map_recv.at[other], **at(line + other, head),
            ).wait_recv()
        m = [(maps_ref[i, 0], maps_ref[i, 1]) for i in range(LINE)]
        (p1,) = compose([m[1]], m[0])
        (q23,) = compose([m[3]], m[2])
        (q45,) = compose([m[5]], m[4])
        (q67,) = compose([m[7]], m[6])
        p2, p3 = compose([m[2], q23], p1)
        q46, q47 = compose([m[6], q67], q45)
        p4, p5, p6, p7 = compose([m[4], q45, q46, q47], p3)
        total_ref[0] = p7[0]
        total_ref[1] = p7[1]
        for i, (t, f) in enumerate((m[0], p1, p2, p3, p4, p5, p6, p7)):
            pre_t_ref[i * W : (i + 1) * W] = lhs_of(t)
            pre_f_ref[i] = f

        @pl.when(x == 0)
        def _():
            line_copy(total_ref.at[1], line_ref, 0, 0, 1).start()

        @pl.when(x == 2)
        def _():
            line_copy(total_ref, far_ref, 0, 1, 3).start()

        @pl.when(x > 0)
        def _():
            line_copy(total_ref.at[1], line_ref, 0, 0, 1).wait_recv()

        @pl.when(x == 1)
        def _():
            next_ref[...] = mm(pre_t_ref[7 * W :], rhs_of(line_ref[...])) + pre_f_ref[7]
            line_copy(next_ref, line_ref, 0, 0, 3).start()
            line_copy(next_ref, line_ref, 1, 0, 2).start()

        @pl.when(x == 3)
        def _():
            line_copy(total_ref, far_ref, 0, 1, 3).wait_recv()
            next_ref[...] = mm(lhs_of(far_ref[0]), rhs_of(line_ref[...])) + far_ref[1]

        @pl.when(x == 0)
        def _():
            given_ref[0] = jnp.zeros((W, W), F32)
            for i in range(1, LINE):
                given_ref[i] = pre_f_ref[i - 1]

        @pl.when(x > 0)
        def _():
            begin = jnp.where(x == 3, next_ref[...], line_ref[...])
            after = mm(pre_t_ref[: 7 * W], rhs_of(begin))
            given_ref[0] = begin
            for i in range(1, LINE):
                given_ref[i] = after[(i - 1) * W : i * W] + pre_f_ref[i - 1]

        for i in (4, 5, 3, 6, 2, 7, 1):
            other = lax.rem(z + i, LINE)
            pltpu.make_async_remote_copy(
                src_ref=given_ref.at[other], dst_ref=start_ref.at[mine],
                send_sem=start_send.at[i], recv_sem=start_recv.at[mine], **at(line + other, head),
            ).start()
        start_ref[mine] = given_ref[z]

    for h in range(HEADS):
        @pl.when(z != 2 * h)
        def _():
            pltpu.make_async_remote_copy(
                src_ref=given_ref.at[0], dst_ref=start_ref.at[h],
                send_sem=start_send.at[0], recv_sem=start_recv.at[h], **at(line + 2 * h, head),
            ).wait_recv()

        heads_out = lo_ref[h] + mm(lq_ref[h], rhs_of(start_ref[h]))
        mean = jnp.sum(heads_out * heads_out, axis=1, keepdims=True) * (1.0 / W)
        normed = heads_out / jnp.sqrt(mean + 1e-5)
        gated_ref[:, :, h * W : (h + 1) * W] = (
            (normed * act_ref[:, h * W : (h + 1) * W]).astype(BF16).reshape(2 * RING, 16, W)
        )

    w_copy.wait()
    block = [lax.rem(y + i, RING) * 2 for i in range(RING)]
    rows = jnp.concatenate(
        [gated_ref[b + 1 - core] for b in block] + [gated_ref[b + core] for b in block], axis=0
    )
    width = w_ref.shape[1] // CHUNKS

    def pair_copy(c):
        return pltpu.make_async_remote_copy(
            src_ref=pair_out.at[c], dst_ref=pair_in.at[c],
            send_sem=pair_send.at[c], recv_sem=pair_recv.at[c], **at(seq, sibling),
        )

    order = (0, 2, 1, 3)
    for c in order:
        part = jnp.dot(rows, w_ref[:, c * width : (c + 1) * width], preferred_element_type=F32)
        pair_out[c] = part[:64].reshape(RING, 16, width)
        pair_copy(c).start()
        own_ref[c] = part[64:].reshape(RING, 16, width)

    def ring_copy(kind, c, src, dst, to):
        return pltpu.make_async_remote_copy(
            src_ref=src, dst_ref=dst, send_sem=ring_send.at[kind, c], recv_sem=ring_recv.at[kind, c],
            **at(seq, to),
        )

    def relay_copy(c):
        return ring_copy(0, c, own_ref.at[c, 2], relay_in.at[c], up if c < 2 else down)

    def up_copy(c):
        return ring_copy(1, c, own_ref.at[c, 1], side_in.at[0, c], up)

    def down_copy(c):
        return ring_copy(2, c, own_ref.at[c, 3], side_in.at[1, c], down)

    for c in order:
        pair_copy(c).wait_recv()
        own_ref[c] = own_ref[c] + pair_in[c]
        relay_copy(c).start()
        (down_copy if c < 2 else up_copy)(c).start()
    for c in order:
        relay_copy(c).wait_recv()
        if c < 2:
            own_ref[c, 1] = own_ref[c, 1] + relay_in[c]
            up_copy(c).start()
        else:
            own_ref[c, 3] = own_ref[c, 3] + relay_in[c]
            down_copy(c).start()
    for c in order:
        up_copy(c).wait_recv()
        down_copy(c).wait_recv()
        out_ref[:, c * width : (c + 1) * width] = (
            own_ref[c, 0] + side_in[0, c] + side_in[1, c]
        ).astype(BF16)

    for h in range(HEADS):
        @pl.when(z != 2 * h)
        def _():
            map_copy(h).wait_send()

    @pl.when(owner)
    def _():
        @pl.when(x == 0)
        def _():
            line_copy(total_ref.at[1], line_ref, 0, 0, 1).wait_send()

        @pl.when(x == 2)
        def _():
            line_copy(total_ref, far_ref, 0, 1, 3).wait_send()

        @pl.when(x == 1)
        def _():
            line_copy(next_ref, line_ref, 0, 0, 3).wait_send()
            line_copy(next_ref, line_ref, 1, 0, 2).wait_send()

        for i in range(1, LINE):
            other = lax.rem(z + i, LINE)
            pltpu.make_async_remote_copy(
                src_ref=given_ref.at[other], dst_ref=start_ref.at[mine],
                send_sem=start_send.at[i], recv_sem=start_recv.at[mine], **at(line + other, head),
            ).wait_send()

    for c in order:
        pair_copy(c).wait_send()
        relay_copy(c).wait_send()
        up_copy(c).wait_send()
        down_copy(c).wait_send()


def on_device(queries, key_vecs, values, out_gate, beta_rates, log_decay, norm_gain, w_out):
    inner, outer = w_out.shape
    width = outer // CHUNKS
    vmem = pl.BlockSpec(memory_space=pltpu.VMEM)
    dma = pltpu.SemaphoreType.DMA
    square = (W, W)
    return pl.pallas_call(
        layer_kernel,
        name="layer",
        out_shape=jax.ShapeDtypeStruct((16, outer), BF16),
        in_specs=[vmem] * 7 + [pl.BlockSpec(memory_space=pl.ANY)],
        out_specs=vmem,
        scratch_shapes=[
            pltpu.VMEM((inner, outer), BF16),
            pltpu.VMEM((HEADS, 2) + square, F32),
            pltpu.VMEM((HEADS, 2 * MICRO, 4 * W), BF16),
            pltpu.VMEM((HEADS,) + square, F32),
            pltpu.VMEM((HEADS, W, 2 * W), BF16),
            pltpu.VMEM((W, inner), F32),
            pltpu.VMEM((LINE, 2) + square, F32),
            pltpu.VMEM((LINE * W, 2 * W), BF16),
            pltpu.VMEM((LINE,) + square, F32),
            pltpu.VMEM((2,) + square, F32),
            pltpu.VMEM((2,) + square, F32),
            pltpu.VMEM(square, F32),
            pltpu.VMEM(square, F32),
            pltpu.VMEM((LINE,) + square, F32),
            pltpu.VMEM((HEADS,) + square, F32),
            pltpu.VMEM((2 * RING, 16, inner), BF16),
            pltpu.VMEM((CHUNKS, RING, 16, width), F32),
            pltpu.VMEM((CHUNKS, RING, 16, width), F32),
            pltpu.VMEM((CHUNKS, RING, 16, width), F32),
            pltpu.VMEM((CHUNKS, 16, width), F32),
            pltpu.VMEM((2, CHUNKS, 16, width), F32),
            dma,
            dma((HEADS,)),
            dma((LINE,)),
            dma((2,)),
            dma((2,)),
            dma((LINE,)),
            dma((HEADS,)),
            dma((CHUNKS,)),
            dma((CHUNKS,)),
            dma((3, CHUNKS)),
            dma((3, CHUNKS)),
        ],
        compiler_params=pltpu.CompilerParams(
            collective_id=0, has_side_effects=True, vmem_limit_bytes=56 * 1024 * 1024
        ),
    )(
        queries,
        key_vecs.reshape(MICRO, inner),
        values.reshape(MICRO, inner),
        out_gate,
        beta_rates,
        log_decay,
        norm_gain.reshape(1, W),
        w_out,
    )


def solution(mesh):
    placed = (
        P("seq", "head"),
        P("seq", None, "head"),
        P("seq", None, "head"),
        P("seq", "head"),
        P(None, "head", "seq"),
        P("head", "seq"),
        P(),
        P("head", None),
    )
    return jax.shard_map(
        on_device, mesh=mesh, in_specs=placed, out_specs=P(("seq", "head"), None), check_vma=False
    )
```

time: 616 us -> 77.4 us (0.13)
  waiting for transfers between devices: 314 us -> 0 us
  other arithmetic: 166 us -> 0 us
  Pallas kernels: 0 us -> 70.8 us
  starting transfers between devices: 60.9 us -> 0 us
  matrix products: 34.2 us -> 0 us
  local copies, waits for them, and re-layouts: 22.6 us -> 6.39 us
  between operations: 13.8 us -> 0.01 us
    ppermute x31 -> x0, waiting for transfers between devices: 252 us -> none  [shifted(): return lax.ppermute(value, axis, pairs)]
    another operation x9 -> x0, other arithmetic: 161 us -> none  [the longest x6 158 us: on_device(): jax.scipy.linalg.solve_triangular(system, right_side, lower=True, unit_di...]
    pallas_call x0 -> x1, Pallas kernels: none -> 70.8 us  [on_device(): pl.pallas_call(layer_kernel, name='layer', out_shape=jax.ShapeDtypeStruct...]
    reduce_scatter x1 -> x0, waiting for transfers between devices: 62 us -> none  [on_device(): lax.psum_scatter(jnp.dot(gated, w_out, preferred_element_type=jnp.float32...]
    ppermute x31 -> x0, starting transfers between devices: 60.9 us -> none  [shifted(): return lax.ppermute(value, axis, pairs)]
    dot_general x46 -> x0, matrix products: 30.8 us -> none  [the longest x37 16.2 us: chain_product(): jnp.einsum('hde,hef->hdf', left_mat, right_mat, precision=full_precision)]
    while x68 -> x0, local copies, waits for them, and re-layouts: 11.7 us -> none
  transfers between devices with their start and end apart: 32 -> 0, of which waited for: 32 -> 0; matrix products, arithmetic and copies ran while one was open for 0% -> 0% of each run, Pallas kernels for 0% -> 0%
where the time goes in v1:
time: 77.4 us; the launch traced here: 77.2 us
  Pallas kernels  70.8 us (91%)
  local copies, waits for them, and re-layouts  6.39 us (8%)
    pallas_call x1, Pallas kernels, on_device(): pl.pallas_call(layer_kernel, name='layer', out_shape=jax.ShapeDtypeStruct...  70.8 us
    unnamed x3, local copies, waits for them, and re-layouts  4.24 us

profile of v1, /device:TPU:7, one launch (start us, length us, event | category | flops | bytes accessed | tf_op | source)
XLA Modules:
  0.0 77.2 jit_solution(6613470053662914518)
XLA Ops:
  0.0 1.3 %copy.11 = bf16[128,3,512]{2,1,0:T(4,128)(2,1)S(1)} copy(bf16[128,3,512]{2,0,1:T(8,128)(2,1)} %param.9) | data formatting | bytes 786432 | tf_op args[1]
  1.3 1.1 %reshape.9.k_ref = bf16[384,512]{1,0:T(8,128)(2,1)} reshape(bf16[128,3,512]{2,1,0:T(4,128)(2,1)S(1)} %copy.11) | data formatting | bytes 786432 | tf_op jit(solution)/shard_map/reshape | solution.py:468
  2.4 1.3 %copy.12 = bf16[128,3,512]{2,1,0:T(4,128)(2,1)S(1)} copy(bf16[128,3,512]{2,0,1:T(8,128)(2,1)} %param.10) | data formatting | bytes 786432 | tf_op args[2]
  3.7 1.1 %reshape.10.v_ref = bf16[384,512]{1,0:T(8,128)(2,1)} reshape(bf16[128,3,512]{2,1,0:T(4,128)(2,1)S(1)} %copy.12) | data formatting | bytes 786432 | tf_op jit(solution)/shard_map/reshape | solution.py:469
  4.8 70.8 %layer.1 = bf16[16,4096]{1,0:T(8,128)(2,1)} custom-call(bf16[128,512]{1,0:T(8,128)(2,1)} %q_ref.1, bf16[384,512]{1,0:T(8,128)(2,1)} %reshape.9.k_ref, bf16[384,512]{1,0:T(8,128)(2,1)} %reshape.10.v_ref, bf16[128,512]{1,0:T(8,128)(2,1)} %gate_ref.1, f32[3,4,128]{2,1,0:T(4,128)} %beta_ref.1, f32[4,128]{1,0:T(4,128)} %decay_ref.1, f32[1,128]{1,0:T(1,128)} %bitcast.1, ...), custom_call_target="tpu_custom_call" | custom-call | tf_op jit(solution)/shard_map/layer/pallas_call | solution.py:423
  75.6 1.6 %copy.14 = bf16[16,4096]{1,0:T(8,128)(2,1)} copy(bf16[16,4096]{1,0:T(8,128)(2,1)} %layer.1) | data formatting | bytes 262144

commit v2 on v1

--- a/solution.py
+++ b/solution.py
@@ -184,7 +184,7 @@
 
 def layer_kernel(
     q_ref, k_ref, v_ref, gate_ref, beta_ref, decay_ref, gain_ref, w_hbm, out_ref,
-    w_ref, tf_ref, x_ref, lo_ref, lq_ref, act_ref,
+    w_ref, keys_ref, values_ref, tf_ref, x_ref, lo_ref, lq_ref, act_ref,
     maps_ref, pre_t_ref, pre_f_ref, total_ref, far_ref, line_ref, next_ref, given_ref, start_ref,
     gated_ref, pair_out, pair_in, own_ref, relay_in, side_in,
     w_sem, map_send, map_recv, line_send, line_recv, start_send, start_recv,
@@ -194,6 +194,11 @@
     x, z = seq // LINE, lax.rem(seq, LINE)
     y, core = head // 2, lax.rem(head, 2)
     line = x * LINE
+    owner = lax.rem(z, 2) == core
+    mine = z // 2
+    width = w_ref.shape[1] // CHUNKS
+    order = (0, 2, 1, 3)
+    held = {}
 
     def at(s, h):
         return {"device_id": (s, h), "device_id_type": MESH}
@@ -212,30 +217,12 @@
         pl.semaphore_signal(barrier, inc=1, **at(lax.rem(x + i, ROWS) * LINE + z, head))
     for h in (up, down, sibling):
         pl.semaphore_signal(barrier, inc=1, **at(seq, h))
-    pl.semaphore_wait(barrier, LINE - 1 + ROWS - 1 + 3)
 
     def map_copy(h):
         return pltpu.make_async_remote_copy(
             src_ref=tf_ref.at[h], dst_ref=maps_ref.at[z],
-            send_sem=map_send.at[h], recv_sem=map_recv.at[z], **at(line + 2 * h, head),
-        )
-
-    def emit(h):
-        @pl.when(z != 2 * h)
-        def _():
-            map_copy(h).start()
-
-        @pl.when(z == 2 * h)
-        def _():
-            maps_ref[z] = tf_ref[h]
-
-    g_row, r_rows = local_maps(k_ref, v_ref, beta_ref, decay_ref, tf_ref, x_ref, emit)
-    local_reads(q_ref, k_ref, decay_ref, x_ref, g_row, r_rows, lo_ref, lq_ref)
-    gate = gate_ref[...].astype(F32)
-    act_ref[...] = (gate / (1.0 + jnp.exp(-gate))) * jnp.concatenate([gain_ref[...]] * HEADS, axis=1)
-
-    owner = lax.rem(z, 2) == 0
-    mine = z // 2
+            send_sem=map_send.at[h], recv_sem=map_recv.at[z], **at(line + 2 * h + core, head),
+        )
 
     def line_copy(src, dst, send, recv, to):
         return pltpu.make_async_remote_copy(
@@ -243,94 +230,12 @@
             **at(to * LINE + z, head),
         )
 
-    @pl.when(owner)
-    def _():
-        for i in range(1, LINE):
-            other = lax.rem(z + i, LINE)
-            pltpu.make_async_remote_copy(
-                src_ref=tf_ref.at[0], dst_ref=maps_ref.at[other],
-                send_sem=map_send.at[0], recv_sem=map_recv.at[other], **at(line + other, head),
-            ).wait_recv()
-        m = [(maps_ref[i, 0], maps_ref[i, 1]) for i in range(LINE)]
-        (p1,) = compose([m[1]], m[0])
-        (q23,) = compose([m[3]], m[2])
-        (q45,) = compose([m[5]], m[4])
-        (q67,) = compose([m[7]], m[6])
-        p2, p3 = compose([m[2], q23], p1)
-        q46, q47 = compose([m[6], q67], q45)
-        p4, p5, p6, p7 = compose([m[4], q45, q46, q47], p3)
-        total_ref[0] = p7[0]
-        total_ref[1] = p7[1]
-        for i, (t, f) in enumerate((m[0], p1, p2, p3, p4, p5, p6, p7)):
-            pre_t_ref[i * W : (i + 1) * W] = lhs_of(t)
-            pre_f_ref[i] = f
-
-        @pl.when(x == 0)
-        def _():
-            line_copy(total_ref.at[1], line_ref, 0, 0, 1).start()
-
-        @pl.when(x == 2)
-        def _():
-            line_copy(total_ref, far_ref, 0, 1, 3).start()
-
-        @pl.when(x > 0)
-        def _():
-            line_copy(total_ref.at[1], line_ref, 0, 0, 1).wait_recv()
-
-        @pl.when(x == 1)
-        def _():
-            next_ref[...] = mm(pre_t_ref[7 * W :], rhs_of(line_ref[...])) + pre_f_ref[7]
-            line_copy(next_ref, line_ref, 0, 0, 3).start()
-            line_copy(next_ref, line_ref, 1, 0, 2).start()
-
-        @pl.when(x == 3)
-        def _():
-            line_copy(total_ref, far_ref, 0, 1, 3).wait_recv()
-            next_ref[...] = mm(lhs_of(far_ref[0]), rhs_of(line_ref[...])) + far_ref[1]
-
-        @pl.when(x == 0)
-        def _():
-            given_ref[0] = jnp.zeros((W, W), F32)
-            for i in range(1, LINE):
-                given_ref[i] = pre_f_ref[i - 1]
-
-        @pl.when(x > 0)
-        def _():
-            begin = jnp.where(x == 3, next_ref[...], line_ref[...])
-            after = mm(pre_t_ref[: 7 * W], rhs_of(begin))
-            given_ref[0] = begin
-            for i in range(1, LINE):
-                given_ref[i] = after[(i - 1) * W : i * W] + pre_f_ref[i - 1]
-
-        for i in (4, 5, 3, 6, 2, 7, 1):
-            other = lax.rem(z + i, LINE)
-            pltpu.make_async_remote_copy(
-                src_ref=given_ref.at[other], dst_ref=start_ref.at[mine],
-                send_sem=start_send.at[i], recv_sem=start_recv.at[mine], **at(line + other, head),
-            ).start()
-        start_ref[mine] = given_ref[z]
-
-    for h in range(HEADS):
-        @pl.when(z != 2 * h)
-        def _():
-            pltpu.make_async_remote_copy(
-                src_ref=given_ref.at[0], dst_ref=start_ref.at[h],
-                send_sem=start_send.at[0], recv_sem=start_recv.at[h], **at(line + 2 * h, head),
-            ).wait_recv()
-
-        heads_out = lo_ref[h] + mm(lq_ref[h], rhs_of(start_ref[h]))
-        mean = jnp.sum(heads_out * heads_out, axis=1, keepdims=True) * (1.0 / W)
-        normed = heads_out / jnp.sqrt(mean + 1e-5)
-        gated_ref[:, :, h * W : (h + 1) * W] = (
-            (normed * act_ref[:, h * W : (h + 1) * W]).astype(BF16).reshape(2 * RING, 16, W)
-        )
-
-    w_copy.wait()
-    block = [lax.rem(y + i, RING) * 2 for i in range(RING)]
-    rows = jnp.concatenate(
-        [gated_ref[b + 1 - core] for b in block] + [gated_ref[b + core] for b in block], axis=0
-    )
-    width = w_ref.shape[1] // CHUNKS
+    def start_copy(i, h):
+        other = lax.rem(z + i, LINE)
+        return pltpu.make_async_remote_copy(
+            src_ref=given_ref.at[other], dst_ref=start_ref.at[h],
+            send_sem=start_send.at[i], recv_sem=start_recv.at[h], **at(line + other, head),
+        )
 
     def pair_copy(c):
         return pltpu.make_async_remote_copy(
@@ -338,13 +243,6 @@
             send_sem=pair_send.at[c], recv_sem=pair_recv.at[c], **at(seq, sibling),
         )
 
-    order = (0, 2, 1, 3)
-    for c in order:
-        part = jnp.dot(rows, w_ref[:, c * width : (c + 1) * width], preferred_element_type=F32)
-        pair_out[c] = part[:64].reshape(RING, 16, width)
-        pair_copy(c).start()
-        own_ref[c] = part[64:].reshape(RING, 16, width)
-
     def ring_copy(kind, c, src, dst, to):
         return pltpu.make_async_remote_copy(
             src_ref=src, dst_ref=dst, send_sem=ring_send.at[kind, c], recv_sem=ring_recv.at[kind, c],
@@ -360,58 +258,213 @@
     def down_copy(c):
         return ring_copy(2, c, own_ref.at[c, 3], side_in.at[1, c], down)
 
-    for c in order:
-        pair_copy(c).wait_recv()
-        own_ref[c] = own_ref[c] + pair_in[c]
-        relay_copy(c).start()
-        (down_copy if c < 2 else up_copy)(c).start()
-    for c in order:
-        relay_copy(c).wait_recv()
-        if c < 2:
-            own_ref[c, 1] = own_ref[c, 1] + relay_in[c]
-            up_copy(c).start()
-        else:
-            own_ref[c, 3] = own_ref[c, 3] + relay_in[c]
-            down_copy(c).start()
-    for c in order:
-        up_copy(c).wait_recv()
-        down_copy(c).wait_recv()
-        out_ref[:, c * width : (c + 1) * width] = (
-            own_ref[c, 0] + side_in[0, c] + side_in[1, c]
-        ).astype(BF16)
-
-    for h in range(HEADS):
-        @pl.when(z != 2 * h)
+    def run_maps():
+        to_time = (STEPS * lax.rem(iota((MICRO, MICRO), 1), W) + iota((MICRO, MICRO), 1) // W == iota((MICRO, MICRO), 0)).astype(BF16)
+        for src, dst in ((k_ref, keys_ref), (v_ref, values_ref)):
+            flat = src[...].reshape(MICRO, HEADS * W)
+            dst[...] = jnp.dot(to_time, flat, preferred_element_type=F32).astype(BF16)
+
+        def emit(h):
+            if h == 0:
+                pl.semaphore_wait(barrier, LINE - 1 + ROWS - 1 + 3)
+
+            @pl.when(z != 2 * h + core)
+            def _():
+                map_copy(h).start()
+
+            @pl.when(z == 2 * h + core)
+            def _():
+                maps_ref[z] = tf_ref[h]
+
+        held["rows"] = local_maps(keys_ref, values_ref, beta_ref, decay_ref, tf_ref, x_ref, emit)
+
+    def end_maps():
+        for h in range(HEADS):
+            @pl.when(z != 2 * h + core)
+            def _():
+                map_copy(h).wait_send()
+
+    def run_reads():
+        g_row, r_rows = held["rows"]
+        local_reads(q_ref, keys_ref, decay_ref, x_ref, g_row, r_rows, lo_ref, lq_ref)
+        gate = gate_ref[...].astype(F32)
+        act_ref[...] = (gate / (1.0 + jnp.exp(-gate))) * jnp.concatenate(
+            [gain_ref[...]] * HEADS, axis=1
+        )
+
+    def run_gather():
+        @pl.when(owner)
         def _():
-            map_copy(h).wait_send()
-
-    @pl.when(owner)
-    def _():
-        @pl.when(x == 0)
+            for i in range(1, LINE):
+                other = lax.rem(z + i, LINE)
+                pltpu.make_async_remote_copy(
+                    src_ref=tf_ref.at[0], dst_ref=maps_ref.at[other],
+                    send_sem=map_send.at[0], recv_sem=map_recv.at[other], **at(line + other, head),
+                ).wait_recv()
+
+    def run_compose():
+        @pl.when(owner)
         def _():
-            line_copy(total_ref.at[1], line_ref, 0, 0, 1).wait_send()
-
-        @pl.when(x == 2)
+            m = [(maps_ref[i, 0], maps_ref[i, 1]) for i in range(LINE)]
+            (p1,) = compose([m[1]], m[0])
+            (q23,) = compose([m[3]], m[2])
+            (q45,) = compose([m[5]], m[4])
+            (q67,) = compose([m[7]], m[6])
+            p2, p3 = compose([m[2], q23], p1)
+            q46, q47 = compose([m[6], q67], q45)
+            p4, p5, p6, p7 = compose([m[4], q45, q46, q47], p3)
+            total_ref[0] = p7[0]
+            total_ref[1] = p7[1]
+            for i, (t, f) in enumerate((m[0], p1, p2, p3, p4, p5, p6, p7)):
+                pre_t_ref[i * W : (i + 1) * W] = lhs_of(t)
+                pre_f_ref[i] = f
+
+    def run_lines():
+        @pl.when(owner)
         def _():
-            line_copy(total_ref, far_ref, 0, 1, 3).wait_send()
-
-        @pl.when(x == 1)
+            @pl.when(x == 0)
+            def _():
+                line_copy(total_ref.at[1], line_ref, 0, 0, 1).start()
+
+            @pl.when(x == 2)
+            def _():
+                line_copy(total_ref, far_ref, 0, 1, 3).start()
+
+            @pl.when(x > 0)
+            def _():
+                line_copy(total_ref.at[1], line_ref, 0, 0, 1).wait_recv()
+
+            @pl.when(x == 1)
+            def _():
+                next_ref[...] = mm(pre_t_ref[7 * W :], rhs_of(line_ref[...])) + pre_f_ref[7]
+                line_copy(next_ref, line_ref, 0, 0, 3).start()
+                line_copy(next_ref, line_ref, 1, 0, 2).start()
+
+            @pl.when(x == 3)
+            def _():
+                line_copy(total_ref, far_ref, 0, 1, 3).wait_recv()
+                next_ref[...] = mm(lhs_of(far_ref[0]), rhs_of(line_ref[...])) + far_ref[1]
+
+            @pl.when(x == 0)
+            def _():
+                given_ref[0] = jnp.zeros((W, W), F32)
+                for i in range(1, LINE):
+                    given_ref[i] = pre_f_ref[i - 1]
+
+            @pl.when(x > 0)
+            def _():
+                begin = jnp.where(x == 3, next_ref[...], line_ref[...])
+                after = mm(pre_t_ref[: 7 * W], rhs_of(begin))
+                given_ref[0] = begin
+                for i in range(1, LINE):
+                    given_ref[i] = after[(i - 1) * W : i * W] + pre_f_ref[i - 1]
+
+    def end_lines():
+        @pl.when(owner)
         def _():
-            line_copy(next_ref, line_ref, 0, 0, 3).wait_send()
-            line_copy(next_ref, line_ref, 1, 0, 2).wait_send()
-
-        for i in range(1, LINE):
-            other = lax.rem(z + i, LINE)
-            pltpu.make_async_remote_copy(
-                src_ref=given_ref.at[other], dst_ref=start_ref.at[mine],
-                send_sem=start_send.at[i], recv_sem=start_recv.at[mine], **at(line + other, head),
-            ).wait_send()
-
-    for c in order:
-        pair_copy(c).wait_send()
-        relay_copy(c).wait_send()
-        up_copy(c).wait_send()
-        down_copy(c).wait_send()
+            @pl.when(x == 0)
+            def _():
+                line_copy(total_ref.at[1], line_ref, 0, 0, 1).wait_send()
+
+            @pl.when(x == 2)
+            def _():
+                line_copy(total_ref, far_ref, 0, 1, 3).wait_send()
+
+            @pl.when(x == 1)
+            def _():
+                line_copy(next_ref, line_ref, 0, 0, 3).wait_send()
+                line_copy(next_ref, line_ref, 1, 0, 2).wait_send()
+
+    def run_starts():
+        @pl.when(owner)
+        def _():
+            for i in (4, 5, 3, 6, 2, 7, 1):
+                start_copy(i, mine).start()
+            start_ref[mine] = given_ref[z]
+
+        for h in range(HEADS):
+            @pl.when(z != 2 * h + core)
+            def _():
+                start_copy(1, h).wait_recv()
+
+    def end_starts():
+        @pl.when(owner)
+        def _():
+            for i in range(1, LINE):
+                start_copy(i, mine).wait_send()
+
+    def run_gated():
+        for h in range(HEADS):
+            heads_out = lo_ref[h] + mm(lq_ref[h], rhs_of(start_ref[h]))
+            mean = jnp.sum(heads_out * heads_out, axis=1, keepdims=True) * (1.0 / W)
+            normed = heads_out / jnp.sqrt(mean + 1e-5)
+            gated_ref[:, :, h * W : (h + 1) * W] = (
+                (normed * act_ref[:, h * W : (h + 1) * W]).astype(BF16).reshape(2 * RING, 16, W)
+            )
+
+    def run_project():
+        w_copy.wait()
+        block = [lax.rem(y + i, RING) * 2 for i in range(RING)]
+        rows = jnp.concatenate(
+            [gated_ref[b + 1 - core] for b in block] + [gated_ref[b + core] for b in block], axis=0
+        )
+        for c in order:
+            part = jnp.dot(rows, w_ref[:, c * width : (c + 1) * width], preferred_element_type=F32)
+            pair_out[c] = part[:64].reshape(RING, 16, width)
+            pair_copy(c).start()
+            own_ref[c] = part[64:].reshape(RING, 16, width)
+
+    def run_pair():
+        for c in order:
+            pair_copy(c).wait_recv()
+            own_ref[c] = own_ref[c] + pair_in[c]
+
+    def end_pair():
+        for c in order:
+            pair_copy(c).wait_send()
+
+    def run_ring():
+        for c in order:
+            relay_copy(c).start()
+            (down_copy if c < 2 else up_copy)(c).start()
+        for c in order:
+            relay_copy(c).wait_recv()
+            if c < 2:
+                own_ref[c, 1] = own_ref[c, 1] + relay_in[c]
+                up_copy(c).start()
+            else:
+                own_ref[c, 3] = own_ref[c, 3] + relay_in[c]
+                down_copy(c).start()
+        for c in order:
+            up_copy(c).wait_recv()
+            down_copy(c).wait_recv()
+            out_ref[:, c * width : (c + 1) * width] = (
+                own_ref[c, 0] + side_in[0, c] + side_in[1, c]
+            ).astype(BF16)
+
+    def end_ring():
+        for c in order:
+            relay_copy(c).wait_send()
+            up_copy(c).wait_send()
+            down_copy(c).wait_send()
+
+    phases = (
+        (run_maps, end_maps),
+        (run_reads, None),
+        (run_gather, None),
+        (run_compose, None),
+        (run_lines, end_lines),
+        (run_starts, end_starts),
+        (run_gated, None),
+        (run_project, end_pair),
+        (run_pair, None),
+        (run_ring, end_ring),
+    )
+    for run, end in phases:
+        run()
+    for run, end in phases:
+        if end is not None:
+            end()
 
 
 def on_device(queries, key_vecs, values, out_gate, beta_rates, log_decay, norm_gain, w_out):
@@ -428,6 +481,8 @@
         out_specs=vmem,
         scratch_shapes=[
             pltpu.VMEM((inner, outer), BF16),
+            pltpu.VMEM((MICRO, inner), BF16),
+            pltpu.VMEM((MICRO, inner), BF16),
             pltpu.VMEM((HEADS, 2) + square, F32),
             pltpu.VMEM((HEADS, 2 * MICRO, 4 * W), BF16),
             pltpu.VMEM((HEADS,) + square, F32),
@@ -465,8 +520,8 @@
         ),
     )(
         queries,
-        key_vecs.reshape(MICRO, inner),
-        values.reshape(MICRO, inner),
+        key_vecs.transpose(1, 0, 2),
+        values.transpose(1, 0, 2),
         out_gate,
         beta_rates,
         log_decay,

time: 77.4 us -> 61.6 us (0.80)
  Pallas kernels: 70.8 us -> 59.9 us
  local copies, waits for them, and re-layouts: 6.39 us -> 1.57 us
    pallas_call x1, Pallas kernels: 70.8 us -> 59.9 us  [on_device(): pl.pallas_call(layer_kernel, name='layer', out_shape=jax.ShapeDtypeStruct...]
    unnamed x3 -> x1, local copies, waits for them, and re-layouts: 4.24 us -> 1.57 us
    reshape x2 -> x0, local copies, waits for them, and re-layouts: 2.15 us -> none  [the longest x1 1.08 us: on_device(): values.reshape(MICRO, inner)]
where the time goes in v2:
time: 61.6 us; the launch traced here: 61.5 us
  Pallas kernels  59.9 us (97%)
  local copies, waits for them, and re-layouts  1.57 us (3%)
    pallas_call x1, Pallas kernels, on_device(): pl.pallas_call(layer_kernel, name='layer', out_shape=jax.ShapeDtypeStruct...  59.9 us
    unnamed x1, local copies, waits for them, and re-layouts  1.57 us

profile of v2, /device:TPU:7, one launch (start us, length us, event | category | flops | bytes accessed | tf_op | source)
XLA Modules:
  0.0 61.5 jit_solution(2123856723057421605)
XLA Ops:
  0.0 59.9 %layer.1 = bf16[16,4096]{1,0:T(8,128)(2,1)} custom-call(bf16[128,512]{1,0:T(8,128)(2,1)} %q_ref.1, bf16[3,128,512]{2,1,0:T(8,128)(2,1)} %bitcast.3, bf16[3,128,512]{2,1,0:T(8,128)(2,1)} %bitcast.4, bf16[128,512]{1,0:T(8,128)(2,1)} %gate_ref.1, f32[3,4,128]{2,1,0:T(4,128)} %beta_ref.1, f32[4,128]{1,0:T(4,128)} %decay_ref.1, f32[1,128]{1,0:T(1,128)} %bitcast.5, ...), custom_call_target="tpu_custom_call" | custom-call | tf_op jit(solution)/shard_map/layer/pallas_call | solution.py:476
  60.0 1.6 %copy.10 = bf16[16,4096]{1,0:T(8,128)(2,1)} copy(bf16[16,4096]{1,0:T(8,128)(2,1)} %layer.1) | data formatting | bytes 262144

commit v3 on v2

--- a/solution.py
+++ b/solution.py
@@ -14,6 +14,7 @@
 STEPS = 3
 MICRO = STEPS * W
 HEADS = 4
+GROUP = 4
 BASE = 32
 LINE = 8
 ROWS = 4
@@ -114,45 +115,55 @@
     same64 = (row_i // 64) == (col_i // 64)
     low32 = same64 & jnp.logical_not(same32)
     low64 = jnp.logical_not(same64)
-    for h in range(HEADS):
-        wide = k_ref[:, h * W : (h + 1) * W].astype(F32)
-        inverse = []
-        for i in range(3):
-            n = h * 3 + i
-            tile = jnp.concatenate([small[s][n] for s in range(BASE // 8)], axis=0)
-            inv = jnp.where(same32, jnp.concatenate([tile] * (W // BASE), axis=0), 0.0)
-            for low in (low32, low64):
-                step = mm(lhs_of(inv), rhs_of(jnp.where(low, systems[h][i, i], 0.0)))
-                inv = inv - mm(lhs_of(step), rhs_of(inv))
-            inverse.append(lhs_of(inv))
-        b_c, g_c = b_col[:, h : h + 1], g_col[:, h : h + 1]
-        right = jnp.concatenate(
-            [
-                b_c * v_ref[:, h * W : (h + 1) * W].astype(F32),
-                (b_c * jnp.exp(g_c) * r_cols[h]) * wide,
-            ],
-            axis=1,
-        )
-        x1 = mm(inverse[0], rhs_of(right[:W]))
-        x1r = rhs_of(x1)
-        x2 = mm(inverse[1], rhs_of(right[W : 2 * W] - mm(lhs_of(systems[h][1, 0]), x1r)))
-        x3 = mm(
-            inverse[2],
-            rhs_of(
-                right[2 * W :]
-                - mm(lhs_of(systems[h][2, 0]), x1r)
-                - mm(lhs_of(systems[h][2, 1]), rhs_of(x2))
-            ),
-        )
-        solved = jnp.concatenate([x1, x2, x3], axis=0)
-        x_ref[h] = rhs_of(solved)
-        g_end = g_col[MICRO - 1 : MICRO, h : h + 1]
-        tail = jnp.concatenate(split((r_cols[h] * jnp.exp(g_end - g_c)) * solved), axis=1)
-        out = jnp.dot(wide.T.astype(BF16), tail, preferred_element_type=F32)
-        out = out[:, : 2 * W] + out[:, 2 * W :]
-        tf_ref[h, 0] = jnp.exp(g_end) * eye - out[:, W:]
-        tf_ref[h, 1] = out[:, :W]
-        emit(h)
+    for group in range(0, HEADS, GROUP):
+        heads = range(group, group + GROUP)
+        inverse = {}
+        for h in heads:
+            for i in range(3):
+                n = h * 3 + i
+                tile = jnp.concatenate([small[s][n] for s in range(BASE // 8)], axis=0)
+                inverse[h, i] = jnp.where(same32, jnp.concatenate([tile] * (W // BASE), axis=0), 0.0)
+        for low in (low32, low64):
+            step = {
+                n: mm(lhs_of(inv), rhs_of(jnp.where(low, systems[n[0]][n[1], n[1]], 0.0)))
+                for n, inv in inverse.items()
+            }
+            inverse = {n: inv - mm(lhs_of(step[n]), rhs_of(inv)) for n, inv in inverse.items()}
+        wide, right, x1, x1r, x2, x3, solved = {}, {}, {}, {}, {}, {}, {}
+        for h in heads:
+            b_c, g_c = b_col[:, h : h + 1], g_col[:, h : h + 1]
+            wide[h] = k_ref[:, h * W : (h + 1) * W].astype(F32)
+            right[h] = jnp.concatenate(
+                [
+                    b_c * v_ref[:, h * W : (h + 1) * W].astype(F32),
+                    (b_c * jnp.exp(g_c) * r_cols[h]) * wide[h],
+                ],
+                axis=1,
+            )
+        for h in heads:
+            x1[h] = mm(lhs_of(inverse[h, 0]), rhs_of(right[h][:W]))
+        for h in heads:
+            x1r[h] = rhs_of(x1[h])
+            x2[h] = right[h][W : 2 * W] - mm(lhs_of(systems[h][1, 0]), x1r[h])
+        for h in heads:
+            x2[h] = mm(lhs_of(inverse[h, 1]), rhs_of(x2[h]))
+        for h in heads:
+            x3[h] = right[h][2 * W :] - mm(lhs_of(systems[h][2, 0]), x1r[h])
+        for h in heads:
+            x3[h] = x3[h] - mm(lhs_of(systems[h][2, 1]), rhs_of(x2[h]))
+        for h in heads:
+            x3[h] = mm(lhs_of(inverse[h, 2]), rhs_of(x3[h]))
+        for h in heads:
+            solved = jnp.concatenate([x1[h], x2[h], x3[h]], axis=0)
+            x_ref[h] = rhs_of(solved)
+            g_c, g_end = g_col[:, h : h + 1], g_col[MICRO - 1 : MICRO, h : h + 1]
+            tail = jnp.concatenate(split((r_cols[h] * jnp.exp(g_end - g_c)) * solved), axis=1)
+            out = jnp.dot(wide[h].T.astype(BF16), tail, preferred_element_type=F32)
+            out = out[:, : 2 * W] + out[:, 2 * W :]
+            tf_ref[h, 0] = jnp.exp(g_end) * eye - out[:, W:]
+            tf_ref[h, 1] = out[:, :W]
+        for h in heads:
+            emit(h)
     return g_row, r_rows
 
 
@@ -161,14 +172,15 @@
     upto = (iota((W, W), 1) <= iota((W, W), 0)).astype(F32)
     q_col = nt(upto, decay, EXACT)
     visible = iota((W, MICRO), 1) <= STEPS * iota((W, MICRO), 0) + STEPS - 1
-    for h in range(HEADS):
-        keys = k_ref[:, h * W : (h + 1) * W]
-        query = q_ref[:, h * W : (h + 1) * W]
-        gap = jnp.where(visible, q_col[:, h : h + 1] - g_row[h : h + 1, :], 0.0)
-        scores = jnp.where(visible, nt(query, keys) * (r_rows[h] * jnp.exp(gap)), 0.0)
-        reads = mm(lhs_of(scores), x_ref[h])
-        lo_ref[h] = reads[:, :W]
-        lq_ref[h] = lhs_of(jnp.exp(q_col[:, h : h + 1]) * query.astype(F32) - reads[:, W:])
+    heads = range(HEADS)
+    query = [q_ref[:, h * W : (h + 1) * W] for h in heads]
+    scores = [nt(query[h], k_ref[:, h * W : (h + 1) * W]) for h in heads]
+    gaps = [jnp.where(visible, q_col[:, h : h + 1] - g_row[h : h + 1, :], 0.0) for h in heads]
+    scores = [jnp.where(visible, scores[h] * (r_rows[h] * jnp.exp(gaps[h])), 0.0) for h in heads]
+    reads = [mm(lhs_of(scores[h]), x_ref[h]) for h in heads]
+    for h in heads:
+        lo_ref[h] = reads[h][:, :W]
+        lq_ref[h] = lhs_of(jnp.exp(q_col[:, h : h + 1]) * query[h].astype(F32) - reads[h][:, W:])
 
 
 def compose(lefts, right):
@@ -194,8 +206,8 @@
     x, z = seq // LINE, lax.rem(seq, LINE)
     y, core = head // 2, lax.rem(head, 2)
     line = x * LINE
-    owner = lax.rem(z, 2) == core
-    mine = z // 2
+    owner = core == 1
+    mine, mine_core = z // 2, lax.rem(z, 2)
     width = w_ref.shape[1] // CHUNKS
     order = (0, 2, 1, 3)
     held = {}
@@ -203,6 +215,7 @@
     def at(s, h):
         return {"device_id": (s, h), "device_id_type": MESH}
 
+    owners, served = y * 2 + 1, y * 2 + mine_core
     up = lax.rem(y + 1, RING) * 2 + core
     down = lax.rem(y + RING - 1, RING) * 2 + core
     sibling = y * 2 + 1 - core
@@ -212,7 +225,8 @@
 
     barrier = pltpu.get_barrier_semaphore()
     for i in range(1, LINE):
-        pl.semaphore_signal(barrier, inc=1, **at(line + lax.rem(z + i, LINE), head))
+        for h in (head, sibling):
+            pl.semaphore_signal(barrier, inc=1, **at(line + lax.rem(z + i, LINE), h))
     for i in range(1, ROWS):
         pl.semaphore_signal(barrier, inc=1, **at(lax.rem(x + i, ROWS) * LINE + z, head))
     for h in (up, down, sibling):
@@ -221,7 +235,8 @@
     def map_copy(h):
         return pltpu.make_async_remote_copy(
             src_ref=tf_ref.at[h], dst_ref=maps_ref.at[z],
-            send_sem=map_send.at[h], recv_sem=map_recv.at[z], **at(line + 2 * h + core, head),
+            send_sem=map_send.at[h], recv_sem=map_recv.at[z],
+            **at(line + 2 * h + core, owners),
         )
 
     def line_copy(src, dst, send, recv, to):
@@ -230,11 +245,10 @@
             **at(to * LINE + z, head),
         )
 
-    def start_copy(i, h):
-        other = lax.rem(z + i, LINE)
+    def start_copy(to, h):
         return pltpu.make_async_remote_copy(
-            src_ref=given_ref.at[other], dst_ref=start_ref.at[h],
-            send_sem=start_send.at[i], recv_sem=start_recv.at[h], **at(line + other, head),
+            src_ref=given_ref.at[to], dst_ref=start_ref.at[h],
+            send_sem=start_send.at[to], recv_sem=start_recv.at[h], **at(line + to, served),
         )
 
     def pair_copy(c):
@@ -266,13 +280,15 @@
 
         def emit(h):
             if h == 0:
-                pl.semaphore_wait(barrier, LINE - 1 + ROWS - 1 + 3)
-
-            @pl.when(z != 2 * h + core)
+                pl.semaphore_wait(barrier, 2 * (LINE - 1) + ROWS - 1 + 3)
+
+            keep = owner & (z == 2 * h + 1)
+
+            @pl.when(jnp.logical_not(keep))
             def _():
                 map_copy(h).start()
 
-            @pl.when(z == 2 * h + core)
+            @pl.when(keep)
             def _():
                 maps_ref[z] = tf_ref[h]
 
@@ -280,7 +296,7 @@
 
     def end_maps():
         for h in range(HEADS):
-            @pl.when(z != 2 * h + core)
+            @pl.when(jnp.logical_not(owner & (z == 2 * h + 1)))
             def _():
                 map_copy(h).wait_send()
 
@@ -295,12 +311,18 @@
     def run_gather():
         @pl.when(owner)
         def _():
-            for i in range(1, LINE):
-                other = lax.rem(z + i, LINE)
+            def arrived(other):
                 pltpu.make_async_remote_copy(
                     src_ref=tf_ref.at[0], dst_ref=maps_ref.at[other],
-                    send_sem=map_send.at[0], recv_sem=map_recv.at[other], **at(line + other, head),
+                    send_sem=map_send.at[0], recv_sem=map_recv.at[other], **at(line + other, sibling),
                 ).wait_recv()
+
+            for i in range(1, LINE):
+                arrived(lax.rem(z + i, LINE))
+
+            @pl.when(mine_core == 0)
+            def _():
+                arrived(z)
 
     def run_compose():
         @pl.when(owner)
@@ -325,39 +347,31 @@
             @pl.when(x == 0)
             def _():
                 line_copy(total_ref.at[1], line_ref, 0, 0, 1).start()
+                given_ref[0] = jnp.zeros((W, W), F32)
 
             @pl.when(x == 2)
             def _():
                 line_copy(total_ref, far_ref, 0, 1, 3).start()
 
-            @pl.when(x > 0)
+            @pl.when(x == 1)
             def _():
                 line_copy(total_ref.at[1], line_ref, 0, 0, 1).wait_recv()
-
-            @pl.when(x == 1)
-            def _():
                 next_ref[...] = mm(pre_t_ref[7 * W :], rhs_of(line_ref[...])) + pre_f_ref[7]
                 line_copy(next_ref, line_ref, 0, 0, 3).start()
                 line_copy(next_ref, line_ref, 1, 0, 2).start()
+                given_ref[0] = line_ref[...]
+
+            @pl.when(x == 2)
+            def _():
+                line_copy(total_ref.at[1], line_ref, 0, 0, 1).wait_recv()
+                given_ref[0] = line_ref[...]
 
             @pl.when(x == 3)
             def _():
                 line_copy(total_ref, far_ref, 0, 1, 3).wait_recv()
-                next_ref[...] = mm(lhs_of(far_ref[0]), rhs_of(line_ref[...])) + far_ref[1]
-
-            @pl.when(x == 0)
-            def _():
-                given_ref[0] = jnp.zeros((W, W), F32)
-                for i in range(1, LINE):
-                    given_ref[i] = pre_f_ref[i - 1]
-
-            @pl.when(x > 0)
-            def _():
-                begin = jnp.where(x == 3, next_ref[...], line_ref[...])
-                after = mm(pre_t_ref[: 7 * W], rhs_of(begin))
-                given_ref[0] = begin
-                for i in range(1, LINE):
-                    given_ref[i] = after[(i - 1) * W : i * W] + pre_f_ref[i - 1]
+                far = lhs_of(far_ref[0])
+                line_copy(total_ref.at[1], line_ref, 0, 0, 1).wait_recv()
+                given_ref[0] = mm(far, rhs_of(line_ref[...])) + far_ref[1]
 
     def end_lines():
         @pl.when(owner)
@@ -376,22 +390,48 @@
                 line_copy(next_ref, line_ref, 1, 0, 2).wait_send()
 
     def run_starts():
+        def give(to):
+            keep = (z == to) & (mine_core == 1)
+
+            @pl.when(jnp.logical_not(keep))
+            def _():
+                start_copy(to, mine).start()
+
+            @pl.when(keep)
+            def _():
+                start_ref[mine] = given_ref[to]
+
         @pl.when(owner)
         def _():
-            for i in (4, 5, 3, 6, 2, 7, 1):
-                start_copy(i, mine).start()
-            start_ref[mine] = given_ref[z]
+            give(0)
+            for batch in ((1, 2, 3, 7), (4, 5, 6)):
+                @pl.when(x == 0)
+                def _():
+                    for to in batch:
+                        given_ref[to] = pre_f_ref[to - 1]
+
+                @pl.when(x > 0)
+                def _():
+                    begin = rhs_of(given_ref[0])
+                    after = [mm(pre_t_ref[(to - 1) * W : to * W], begin) for to in batch]
+                    for to, part in zip(batch, after):
+                        given_ref[to] = part + pre_f_ref[to - 1]
+
+                for to in batch:
+                    give(to)
 
         for h in range(HEADS):
-            @pl.when(z != 2 * h + core)
-            def _():
-                start_copy(1, h).wait_recv()
+            @pl.when(jnp.logical_not(owner & (z == 2 * h + 1)))
+            def _():
+                start_copy(0, h).wait_recv()
 
     def end_starts():
         @pl.when(owner)
         def _():
-            for i in range(1, LINE):
-                start_copy(i, mine).wait_send()
+            for to in range(LINE):
+                @pl.when(jnp.logical_not((z == to) & (mine_core == 1)))
+                def _():
+                    start_copy(to, mine).wait_send()
 
     def run_gated():
         for h in range(HEADS):
@@ -414,17 +454,14 @@
             pair_copy(c).start()
             own_ref[c] = part[64:].reshape(RING, 16, width)
 
-    def run_pair():
+    def end_pair():
+        for c in order:
+            pair_copy(c).wait_send()
+
+    def run_ring():
         for c in order:
             pair_copy(c).wait_recv()
             own_ref[c] = own_ref[c] + pair_in[c]
-
-    def end_pair():
-        for c in order:
-            pair_copy(c).wait_send()
-
-    def run_ring():
-        for c in order:
             relay_copy(c).start()
             (down_copy if c < 2 else up_copy)(c).start()
         for c in order:
@@ -457,7 +494,6 @@
         (run_starts, end_starts),
         (run_gated, None),
         (run_project, end_pair),
-        (run_pair, None),
         (run_ring, end_ring),
     )
     for run, end in phases:

time: 61.6 us -> 55.5 us (0.901)
  Pallas kernels: 59.9 us -> 53.9 us
    pallas_call x1, Pallas kernels: 59.9 us -> 53.9 us  [on_device(): pl.pallas_call(layer_kernel, name='layer', out_shape=jax.ShapeDtypeStruct...]
where the time goes in v3:
time: 55.5 us; the launch traced here: 55.4 us
  Pallas kernels  53.9 us (97%)
  local copies, waits for them, and re-layouts  1.57 us (3%)
    pallas_call x1, Pallas kernels, on_device(): pl.pallas_call(layer_kernel, name='layer', out_shape=jax.ShapeDtypeStruct...  53.9 us
    unnamed x1, local copies, waits for them, and re-layouts  1.57 us

profile of v3, /device:TPU:7, one launch (start us, length us, event | category | flops | bytes accessed | tf_op | source)
XLA Modules:
  0.0 55.4 jit_solution(11007899130049455854)
XLA Ops:
  0.0 53.9 %layer.1 = bf16[16,4096]{1,0:T(8,128)(2,1)} custom-call(bf16[128,512]{1,0:T(8,128)(2,1)} %q_ref.1, bf16[3,128,512]{2,1,0:T(8,128)(2,1)} %bitcast.3, bf16[3,128,512]{2,1,0:T(8,128)(2,1)} %bitcast.4, bf16[128,512]{1,0:T(8,128)(2,1)} %gate_ref.1, f32[3,4,128]{2,1,0:T(4,128)} %beta_ref.1, f32[4,128]{1,0:T(4,128)} %decay_ref.1, f32[1,128]{1,0:T(1,128)} %bitcast.5, ...), custom_call_target="tpu_custom_call" | custom-call | tf_op jit(solution)/shard_map/layer/pallas_call | solution.py:512
  53.9 1.6 %copy.10 = bf16[16,4096]{1,0:T(8,128)(2,1)} copy(bf16[16,4096]{1,0:T(8,128)(2,1)} %layer.1) | data formatting | bytes 262144

commit v4 on v3

--- a/solution.py
+++ b/solution.py
@@ -9,13 +9,12 @@
 
 F32 = jnp.float32
 BF16 = jnp.bfloat16
-EXACT = lax.Precision.HIGHEST
 W = 128
 STEPS = 3
 MICRO = STEPS * W
 HEADS = 4
 GROUP = 4
-BASE = 32
+BASE = 16
 LINE = 8
 ROWS = 4
 RING = 4
@@ -32,6 +31,11 @@
     return hi, (a - hi.astype(F32)).astype(BF16)
 
 
+def split3(a):
+    hi, rest = a.astype(BF16), a - a.astype(BF16).astype(F32)
+    return (hi,) + split(rest)
+
+
 def lhs_of(a):
     return jnp.concatenate(split(a), axis=1)
 
@@ -47,21 +51,22 @@
     return out[:, :half] + out[:, half:]
 
 
-def nt(a, b, precision=None):
-    return lax.dot_general(
-        a, b, (((1,), (1,)), ((), ())), preferred_element_type=F32, precision=precision
-    )
-
-
-def local_maps(k_ref, v_ref, beta_ref, decay_ref, tf_ref, x_ref, emit):
-    step_i, token_i = iota((MICRO, W), 0), iota((MICRO, W), 1)
-    upto = (STEPS * token_i <= step_i).astype(F32)
-    decay = jnp.maximum(decay_ref[...], -110.0)
-    g_col = nt(upto, decay, EXACT)
-    g_row = nt(decay, upto, EXACT)
-    b_col = sum(
-        nt((STEPS * token_i + j == step_i).astype(F32), beta_ref[j], EXACT) for j in range(STEPS)
-    )
+def nt(a, b):
+    return lax.dot_general(a, b, (((1,), (1,)), ((), ())), preferred_element_type=F32)
+
+
+def local_maps(raw_ref, v_ref, beta_ref, decay_ref, k_ref, tf_ref, x_ref, v_wait):
+    time_i, flat_i = iota((MICRO, MICRO), 0), iota((MICRO, MICRO), 1)
+    to_time = (STEPS * lax.rem(flat_i, W) + flat_i // W == time_i).astype(BF16)
+    raw = raw_ref[...].reshape(MICRO, HEADS * W)
+    k_ref[...] = jnp.dot(to_time, raw, preferred_element_type=F32).astype(BF16)
+    upto = (STEPS * iota((MICRO, W), 1) <= iota((MICRO, W), 0)).astype(BF16)
+    upto = jnp.concatenate([upto] * 3, axis=1)
+    decay = jnp.concatenate(split3(jnp.maximum(decay_ref[...], -110.0)), axis=1)
+    g_col = nt(upto, decay)
+    g_row = nt(decay, upto)
+    beta = jnp.concatenate([beta_ref[j] for j in range(STEPS)], axis=1)
+    b_col = nt(jnp.concatenate([to_time] * 3, axis=1), jnp.concatenate(split3(beta), axis=1))
     row_i, col_i = iota((W, W), 0), iota((W, W), 1)
     strict = row_i > col_i
     eye = (row_i == col_i).astype(F32)
@@ -111,10 +116,12 @@
         row = small[first][:, j % 8 : j % 8 + 1, :]
         for s in range(first, BASE // 8):
             small[s] = small[s] - factor[:, 8 * s : 8 * s + 8, :] * row
-    same32 = (row_i // 32) == (col_i // 32)
-    same64 = (row_i // 64) == (col_i // 64)
-    low32 = same64 & jnp.logical_not(same32)
-    low64 = jnp.logical_not(same64)
+    same = {n: (row_i // n) == (col_i // n) for n in (16, 32, 64)}
+    lows = {
+        16: same[32] & jnp.logical_not(same[16]),
+        32: same[64] & jnp.logical_not(same[32]),
+        64: jnp.logical_not(same[64]),
+    }
     for group in range(0, HEADS, GROUP):
         heads = range(group, group + GROUP)
         inverse = {}
@@ -122,20 +129,23 @@
             for i in range(3):
                 n = h * 3 + i
                 tile = jnp.concatenate([small[s][n] for s in range(BASE // 8)], axis=0)
-                inverse[h, i] = jnp.where(same32, jnp.concatenate([tile] * (W // BASE), axis=0), 0.0)
-        for low in (low32, low64):
+                inverse[h, i] = jnp.where(same[BASE], jnp.concatenate([tile] * (W // BASE), axis=0), 0.0)
+        for low in [lows[n] for n in (16, 32, 64) if n >= BASE]:
             step = {
                 n: mm(lhs_of(inv), rhs_of(jnp.where(low, systems[n[0]][n[1], n[1]], 0.0)))
                 for n, inv in inverse.items()
             }
             inverse = {n: inv - mm(lhs_of(step[n]), rhs_of(inv)) for n, inv in inverse.items()}
+        v_wait()
         wide, right, x1, x1r, x2, x3, solved = {}, {}, {}, {}, {}, {}, {}
+        values = v_ref[...].reshape(MICRO, HEADS * W)
+        values = jnp.dot(to_time, values, preferred_element_type=F32)
         for h in heads:
             b_c, g_c = b_col[:, h : h + 1], g_col[:, h : h + 1]
             wide[h] = k_ref[:, h * W : (h + 1) * W].astype(F32)
             right[h] = jnp.concatenate(
                 [
-                    b_c * v_ref[:, h * W : (h + 1) * W].astype(F32),
+                    b_c * values[:, h * W : (h + 1) * W],
                     (b_c * jnp.exp(g_c) * r_cols[h]) * wide[h],
                 ],
                 axis=1,
@@ -162,15 +172,13 @@
             out = out[:, : 2 * W] + out[:, 2 * W :]
             tf_ref[h, 0] = jnp.exp(g_end) * eye - out[:, W:]
             tf_ref[h, 1] = out[:, :W]
-        for h in heads:
-            emit(h)
     return g_row, r_rows
 
 
 def local_reads(q_ref, k_ref, decay_ref, x_ref, g_row, r_rows, lo_ref, lq_ref):
-    decay = jnp.maximum(decay_ref[...], -110.0)
-    upto = (iota((W, W), 1) <= iota((W, W), 0)).astype(F32)
-    q_col = nt(upto, decay, EXACT)
+    decay = jnp.concatenate(split3(jnp.maximum(decay_ref[...], -110.0)), axis=1)
+    upto = (iota((W, W), 1) <= iota((W, W), 0)).astype(BF16)
+    q_col = nt(jnp.concatenate([upto] * 3, axis=1), decay)
     visible = iota((W, MICRO), 1) <= STEPS * iota((W, MICRO), 0) + STEPS - 1
     heads = range(HEADS)
     query = [q_ref[:, h * W : (h + 1) * W] for h in heads]
@@ -195,11 +203,11 @@
 
 
 def layer_kernel(
-    q_ref, k_ref, v_ref, gate_ref, beta_ref, decay_ref, gain_ref, w_hbm, out_ref,
-    w_ref, keys_ref, values_ref, tf_ref, x_ref, lo_ref, lq_ref, act_ref,
-    maps_ref, pre_t_ref, pre_f_ref, total_ref, far_ref, line_ref, next_ref, given_ref, start_ref,
+    q_hbm, k_hbm, v_hbm, gate_hbm, beta_ref, decay_ref, gain_ref, w_hbm, out_ref,
+    q_ref, raw_ref, v_ref, gate_ref, w_ref, keys_ref, tf_ref, x_ref, lo_ref, lq_ref, act_ref,
+    maps_ref, pre_t_ref, pre_f_ref, total_ref, far_ref, line_ref, given_ref, start_ref,
     gated_ref, pair_out, pair_in, own_ref, relay_in, side_in,
-    w_sem, map_send, map_recv, line_send, line_recv, start_send, start_recv,
+    in_sem, w_sem, map_send, map_recv, line_send, line_recv, start_send, start_recv,
     pair_send, pair_recv, ring_send, ring_recv,
 ):
     seq, head = lax.axis_index("seq"), lax.axis_index("head")
@@ -209,7 +217,6 @@
     owner = core == 1
     mine, mine_core = z // 2, lax.rem(z, 2)
     width = w_ref.shape[1] // CHUNKS
-    order = (0, 2, 1, 3)
     held = {}
 
     def at(s, h):
@@ -220,8 +227,14 @@
     down = lax.rem(y + RING - 1, RING) * 2 + core
     sibling = y * 2 + 1 - core
 
+    inputs = ((k_hbm, raw_ref), (v_hbm, v_ref), (q_hbm, q_ref), (gate_hbm, gate_ref))
+
+    def in_copy(i):
+        return pltpu.make_async_copy(*inputs[i], in_sem.at[i])
+
+    for i in range(4):
+        in_copy(i).start()
     w_copy = pltpu.make_async_copy(w_hbm, w_ref, w_sem)
-    w_copy.start()
 
     barrier = pltpu.get_barrier_semaphore()
     for i in range(1, LINE):
@@ -257,31 +270,37 @@
             send_sem=pair_send.at[c], recv_sem=pair_recv.at[c], **at(seq, sibling),
         )
 
-    def ring_copy(kind, c, src, dst, to):
+    def ring_copy(kind, c, src, dst, upward):
         return pltpu.make_async_remote_copy(
             src_ref=src, dst_ref=dst, send_sem=ring_send.at[kind, c], recv_sem=ring_recv.at[kind, c],
-            **at(seq, to),
+            **at(seq, jnp.where(upward, up, down)),
         )
 
     def relay_copy(c):
-        return ring_copy(0, c, own_ref.at[c, 2], relay_in.at[c], up if c < 2 else down)
-
-    def up_copy(c):
-        return ring_copy(1, c, own_ref.at[c, 1], side_in.at[0, c], up)
-
-    def down_copy(c):
-        return ring_copy(2, c, own_ref.at[c, 3], side_in.at[1, c], down)
+        return ring_copy(0, c, own_ref.at[c, 2], relay_in.at[c], c < CHUNKS // 2)
+
+    def side_copy(c):
+        part = c // (CHUNKS // 2)
+        return ring_copy(1, c, own_ref.at[c, 3 - 2 * part], side_in.at[1 - part, c], part == 1)
+
+    def onward_copy(c):
+        part = c // (CHUNKS // 2)
+        return ring_copy(2, c, own_ref.at[c, 1 + 2 * part], side_in.at[part, c], part == 0)
+
+    def each_chunk(body):
+        def step(i, carry):
+            body(lax.rem(i, 2) * (CHUNKS // 2) + i // 2)
+            return carry
+
+        lax.fori_loop(0, CHUNKS, step, 0)
 
     def run_maps():
-        to_time = (STEPS * lax.rem(iota((MICRO, MICRO), 1), W) + iota((MICRO, MICRO), 1) // W == iota((MICRO, MICRO), 0)).astype(BF16)
-        for src, dst in ((k_ref, keys_ref), (v_ref, values_ref)):
-            flat = src[...].reshape(MICRO, HEADS * W)
-            dst[...] = jnp.dot(to_time, flat, preferred_element_type=F32).astype(BF16)
-
-        def emit(h):
-            if h == 0:
-                pl.semaphore_wait(barrier, 2 * (LINE - 1) + ROWS - 1 + 3)
-
+        in_copy(0).wait()
+        held["rows"] = local_maps(
+            raw_ref, v_ref, beta_ref, decay_ref, keys_ref, tf_ref, x_ref, in_copy(1).wait
+        )
+        pl.semaphore_wait(barrier, 2 * (LINE - 1) + ROWS - 1 + 3)
+        for h in range(HEADS):
             keep = owner & (z == 2 * h + 1)
 
             @pl.when(jnp.logical_not(keep))
@@ -291,8 +310,6 @@
             @pl.when(keep)
             def _():
                 maps_ref[z] = tf_ref[h]
-
-        held["rows"] = local_maps(keys_ref, values_ref, beta_ref, decay_ref, tf_ref, x_ref, emit)
 
     def end_maps():
         for h in range(HEADS):
@@ -302,6 +319,8 @@
 
     def run_reads():
         g_row, r_rows = held["rows"]
+        in_copy(2).wait()
+        in_copy(3).wait()
         local_reads(q_ref, keys_ref, decay_ref, x_ref, g_row, r_rows, lo_ref, lq_ref)
         gate = gate_ref[...].astype(F32)
         act_ref[...] = (gate / (1.0 + jnp.exp(-gate))) * jnp.concatenate(
@@ -341,53 +360,59 @@
                 pre_t_ref[i * W : (i + 1) * W] = lhs_of(t)
                 pre_f_ref[i] = f
 
+    def run_weights():
+        w_copy.start()
+
     def run_lines():
         @pl.when(owner)
         def _():
             @pl.when(x == 0)
             def _():
-                line_copy(total_ref.at[1], line_ref, 0, 0, 1).start()
+                for i, to in enumerate((3, 1, 2)):
+                    line_copy(total_ref.at[1], line_ref, i, 0, to).start()
                 given_ref[0] = jnp.zeros((W, W), F32)
 
+            @pl.when(x == 1)
+            def _():
+                for i, to in enumerate((3, 2)):
+                    line_copy(total_ref, far_ref.at[0], i, 1, to).start()
+
             @pl.when(x == 2)
             def _():
-                line_copy(total_ref, far_ref, 0, 1, 3).start()
-
-            @pl.when(x == 1)
-            def _():
-                line_copy(total_ref.at[1], line_ref, 0, 0, 1).wait_recv()
-                next_ref[...] = mm(pre_t_ref[7 * W :], rhs_of(line_ref[...])) + pre_f_ref[7]
-                line_copy(next_ref, line_ref, 0, 0, 3).start()
-                line_copy(next_ref, line_ref, 1, 0, 2).start()
-                given_ref[0] = line_ref[...]
-
-            @pl.when(x == 2)
+                line_copy(total_ref, far_ref.at[1], 0, 2, 3).start()
+
+            @pl.when(x > 0)
             def _():
                 line_copy(total_ref.at[1], line_ref, 0, 0, 1).wait_recv()
                 given_ref[0] = line_ref[...]
 
+            @pl.when(x > 1)
+            def _():
+                begin = rhs_of(line_ref[...])
+                line_copy(total_ref, far_ref.at[0], 0, 1, 3).wait_recv()
+                given_ref[0] = mm(lhs_of(far_ref[0, 0]), begin) + far_ref[0, 1]
+
             @pl.when(x == 3)
             def _():
-                line_copy(total_ref, far_ref, 0, 1, 3).wait_recv()
-                far = lhs_of(far_ref[0])
-                line_copy(total_ref.at[1], line_ref, 0, 0, 1).wait_recv()
-                given_ref[0] = mm(far, rhs_of(line_ref[...])) + far_ref[1]
+                line_copy(total_ref, far_ref.at[1], 0, 2, 3).wait_recv()
+                given_ref[0] = mm(lhs_of(far_ref[1, 0]), rhs_of(given_ref[0])) + far_ref[1, 1]
 
     def end_lines():
         @pl.when(owner)
         def _():
             @pl.when(x == 0)
             def _():
-                line_copy(total_ref.at[1], line_ref, 0, 0, 1).wait_send()
+                for i, to in enumerate((3, 1, 2)):
+                    line_copy(total_ref.at[1], line_ref, i, 0, to).wait_send()
+
+            @pl.when(x == 1)
+            def _():
+                for i, to in enumerate((3, 2)):
+                    line_copy(total_ref, far_ref.at[0], i, 1, to).wait_send()
 
             @pl.when(x == 2)
             def _():
-                line_copy(total_ref, far_ref, 0, 1, 3).wait_send()
-
-            @pl.when(x == 1)
-            def _():
-                line_copy(next_ref, line_ref, 0, 0, 3).wait_send()
-                line_copy(next_ref, line_ref, 1, 0, 2).wait_send()
+                line_copy(total_ref, far_ref.at[1], 0, 2, 3).wait_send()
 
     def run_starts():
         def give(to):
@@ -448,52 +473,58 @@
         rows = jnp.concatenate(
             [gated_ref[b + 1 - core] for b in block] + [gated_ref[b + core] for b in block], axis=0
         )
-        for c in order:
-            part = jnp.dot(rows, w_ref[:, c * width : (c + 1) * width], preferred_element_type=F32)
+
+        def project(c):
+            columns = pl.ds(pl.multiple_of(c * width, width), width)
+            part = jnp.dot(rows, w_ref[:, columns], preferred_element_type=F32)
             pair_out[c] = part[:64].reshape(RING, 16, width)
             pair_copy(c).start()
             own_ref[c] = part[64:].reshape(RING, 16, width)
 
-    def end_pair():
-        for c in order:
-            pair_copy(c).wait_send()
+        each_chunk(project)
 
     def run_ring():
-        for c in order:
+        def begin(c):
             pair_copy(c).wait_recv()
             own_ref[c] = own_ref[c] + pair_in[c]
             relay_copy(c).start()
-            (down_copy if c < 2 else up_copy)(c).start()
-        for c in order:
+            side_copy(c).start()
+
+        def forward(c):
             relay_copy(c).wait_recv()
-            if c < 2:
-                own_ref[c, 1] = own_ref[c, 1] + relay_in[c]
-                up_copy(c).start()
-            else:
-                own_ref[c, 3] = own_ref[c, 3] + relay_in[c]
-                down_copy(c).start()
-        for c in order:
-            up_copy(c).wait_recv()
-            down_copy(c).wait_recv()
-            out_ref[:, c * width : (c + 1) * width] = (
-                own_ref[c, 0] + side_in[0, c] + side_in[1, c]
-            ).astype(BF16)
+            block = 1 + 2 * (c // (CHUNKS // 2))
+            own_ref[c, block] = own_ref[c, block] + relay_in[c]
+            onward_copy(c).start()
+
+        def finish(c):
+            side_copy(c).wait_recv()
+            onward_copy(c).wait_recv()
+            columns = pl.ds(pl.multiple_of(c * width, width), width)
+            out_ref[:, columns] = (own_ref[c, 0] + side_in[0, c] + side_in[1, c]).astype(BF16)
+
+        each_chunk(begin)
+        each_chunk(forward)
+        each_chunk(finish)
 
     def end_ring():
-        for c in order:
+        def sent(c):
+            pair_copy(c).wait_send()
             relay_copy(c).wait_send()
-            up_copy(c).wait_send()
-            down_copy(c).wait_send()
+            side_copy(c).wait_send()
+            onward_copy(c).wait_send()
+
+        each_chunk(sent)
 
     phases = (
         (run_maps, end_maps),
         (run_reads, None),
+        (run_weights, None),
         (run_gather, None),
         (run_compose, None),
         (run_lines, end_lines),
         (run_starts, end_starts),
         (run_gated, None),
-        (run_project, end_pair),
+        (run_project, None),
         (run_ring, end_ring),
     )
     for run, end in phases:
@@ -507,17 +538,21 @@
     inner, outer = w_out.shape
     width = outer // CHUNKS
     vmem = pl.BlockSpec(memory_space=pltpu.VMEM)
+    hbm = pl.BlockSpec(memory_space=pl.ANY)
     dma = pltpu.SemaphoreType.DMA
     square = (W, W)
     return pl.pallas_call(
         layer_kernel,
         name="layer",
         out_shape=jax.ShapeDtypeStruct((16, outer), BF16),
-        in_specs=[vmem] * 7 + [pl.BlockSpec(memory_space=pl.ANY)],
+        in_specs=[hbm] * 4 + [vmem] * 3 + [hbm],
         out_specs=vmem,
         scratch_shapes=[
+            pltpu.VMEM((W, inner), BF16),
+            pltpu.VMEM((STEPS, W, inner), BF16),
+            pltpu.VMEM((STEPS, W, inner), BF16),
+            pltpu.VMEM((W, inner), BF16),
             pltpu.VMEM((inner, outer), BF16),
-            pltpu.VMEM((MICRO, inner), BF16),
             pltpu.VMEM((MICRO, inner), BF16),
             pltpu.VMEM((HEADS, 2) + square, F32),
             pltpu.VMEM((HEADS, 2 * MICRO, 4 * W), BF16),
@@ -528,8 +563,7 @@
             pltpu.VMEM((LINE * W, 2 * W), BF16),
             pltpu.VMEM((LINE,) + square, F32),
             pltpu.VMEM((2,) + square, F32),
-            pltpu.VMEM((2,) + square, F32),
-            pltpu.VMEM(square, F32),
+            pltpu.VMEM((2, 2) + square, F32),
             pltpu.VMEM(square, F32),
             pltpu.VMEM((LINE,) + square, F32),
             pltpu.VMEM((HEADS,) + square, F32),
@@ -539,11 +573,12 @@
             pltpu.VMEM((CHUNKS, RING, 16, width), F32),
             pltpu.VMEM((CHUNKS, 16, width), F32),
             pltpu.VMEM((2, CHUNKS, 16, width), F32),
+            dma((4,)),
             dma,
             dma((HEADS,)),
             dma((LINE,)),
-            dma((2,)),
-            dma((2,)),
+            dma((3,)),
+            dma((3,)),
             dma((LINE,)),
             dma((HEADS,)),
             dma((CHUNKS,)),

time: 55.5 us -> 54 us (0.973)
  Pallas kernels: 53.9 us -> 52.2 us
    pallas_call x1, Pallas kernels: 53.9 us -> 52.2 us  [on_device(): pl.pallas_call(layer_kernel, name='layer', out_shape=jax.ShapeDtypeStruct...]
where the time goes in v4:
time: 54 us; the launch traced here: 53.8 us
  Pallas kernels  52.2 us (97%)
  local copies, waits for them, and re-layouts  1.57 us (3%)
    pallas_call x1, Pallas kernels, on_device(): pl.pallas_call(layer_kernel, name='layer', out_shape=jax.ShapeDtypeStruct...  52.2 us
    unnamed x1, local copies, waits for them, and re-layouts  1.57 us

profile of v4, /device:TPU:7, one launch (start us, length us, event | category | flops | bytes accessed | tf_op | source)
XLA Modules:
  0.0 53.8 jit_solution(12773930880148688932)
XLA Ops:
  0.0 52.2 %layer.1 = bf16[16,4096]{1,0:T(8,128)(2,1)} custom-call(bf16[128,512]{1,0:T(8,128)(2,1)} %q_hbm.1, bf16[3,128,512]{2,1,0:T(8,128)(2,1)} %bitcast.3, bf16[3,128,512]{2,1,0:T(8,128)(2,1)} %bitcast.4, bf16[128,512]{1,0:T(8,128)(2,1)} %gate_hbm.1, f32[3,4,128]{2,1,0:T(4,128)} %beta_ref.1, f32[4,128]{1,0:T(4,128)} %decay_ref.1, f32[1,128]{1,0:T(1,128)} %bitcast.5, ...), custom_call_target="tpu_custom_call" | custom-call | tf_op jit(solution)/shard_map/layer/pallas_call | solution.py:544
  52.2 1.6 %copy.10 = bf16[16,4096]{1,0:T(8,128)(2,1)} copy(bf16[16,4096]{1,0:T(8,128)(2,1)} %layer.1) | data formatting | bytes 262144

commit v5 on v4

--- a/solution.py
+++ b/solution.py
@@ -49,6 +49,13 @@
     out = jnp.dot(left, right, preferred_element_type=F32)
     half = out.shape[1] // 2
     return out[:, :half] + out[:, half:]
+
+
+def mm_few(left, right):
+    out = jnp.dot(left, right, preferred_element_type=F32)
+    rows, columns = out.shape[0] // 2, out.shape[1] // 2
+    out = out[:rows] + out[rows:]
+    return out[:, :columns] + out[:, columns:]
 
 
 def nt(a, b):
@@ -116,26 +123,33 @@
         row = small[first][:, j % 8 : j % 8 + 1, :]
         for s in range(first, BASE // 8):
             small[s] = small[s] - factor[:, 8 * s : 8 * s + 8, :] * row
-    same = {n: (row_i // n) == (col_i // n) for n in (16, 32, 64)}
-    lows = {
-        16: same[32] & jnp.logical_not(same[16]),
-        32: same[64] & jnp.logical_not(same[32]),
-        64: jnp.logical_not(same[64]),
-    }
+    row_p, col_p = iota((W, 2 * W), 0), lax.rem(iota((W, 2 * W), 1), W)
+    widths = [n for n in (16, 32, 64) if n >= BASE]
+    same = {n: (row_p // n == col_p // n).astype(F32) for n in widths + [W]}
+    low = {n: (same[2 * n] - same[n]).astype(BF16) for n in widths}
+    same = {n: same[n].astype(BF16) for n in widths}
     for group in range(0, HEADS, GROUP):
         heads = range(group, group + GROUP)
-        inverse = {}
-        for h in heads:
-            for i in range(3):
-                n = h * 3 + i
-                tile = jnp.concatenate([small[s][n] for s in range(BASE // 8)], axis=0)
-                inverse[h, i] = jnp.where(same[BASE], jnp.concatenate([tile] * (W // BASE), axis=0), 0.0)
-        for low in [lows[n] for n in (16, 32, 64) if n >= BASE]:
-            step = {
-                n: mm(lhs_of(inv), rhs_of(jnp.where(low, systems[n[0]][n[1], n[1]], 0.0)))
-                for n, inv in inverse.items()
-            }
-            inverse = {n: inv - mm(lhs_of(step[n]), rhs_of(inv)) for n, inv in inverse.items()}
+        inverse = {
+            (h, i): jnp.concatenate([small[s][h * 3 + i] for s in range(BASE // 8)], axis=0)
+            for h in heads
+            for i in range(3)
+        }
+        below = {n: lhs_of(systems[n[0]][n[1], n[1]]) for n in inverse}
+        for width in widths:
+            even = lax.rem(iota((width, W), 1) // width, 2) == 0
+            left = {n: split(inv) for n, inv in inverse.items()}
+            step = {}
+            for n in inverse:
+                rows = jnp.concatenate(left[n], axis=0)
+                step[n] = mm_few(rows, below[n] * low[width])
+            for n, inv in inverse.items():
+                full = jnp.concatenate([jnp.concatenate(left[n], axis=1)] * (W // width), axis=0)
+                rows = jnp.concatenate(split(step[n]), axis=0)
+                corner = mm_few(rows, full * same[width])
+                inverse[n] = jnp.concatenate(
+                    [jnp.where(even, inv, 0.0), jnp.where(even, -corner, inv)], axis=0
+                )
         v_wait()
         wide, right, x1, x1r, x2, x3, solved = {}, {}, {}, {}, {}, {}, {}
         values = v_ref[...].reshape(MICRO, HEADS * W)
@@ -165,7 +179,7 @@
             x3[h] = mm(lhs_of(inverse[h, 2]), rhs_of(x3[h]))
         for h in heads:
             solved = jnp.concatenate([x1[h], x2[h], x3[h]], axis=0)
-            x_ref[h] = rhs_of(solved)
+            x_ref[h] = solved
             g_c, g_end = g_col[:, h : h + 1], g_col[MICRO - 1 : MICRO, h : h + 1]
             tail = jnp.concatenate(split((r_cols[h] * jnp.exp(g_end - g_c)) * solved), axis=1)
             out = jnp.dot(wide[h].T.astype(BF16), tail, preferred_element_type=F32)
@@ -185,7 +199,7 @@
     scores = [nt(query[h], k_ref[:, h * W : (h + 1) * W]) for h in heads]
     gaps = [jnp.where(visible, q_col[:, h : h + 1] - g_row[h : h + 1, :], 0.0) for h in heads]
     scores = [jnp.where(visible, scores[h] * (r_rows[h] * jnp.exp(gaps[h])), 0.0) for h in heads]
-    reads = [mm(lhs_of(scores[h]), x_ref[h]) for h in heads]
+    reads = [mm(lhs_of(scores[h]), rhs_of(x_ref[h])) for h in heads]
     for h in heads:
         lo_ref[h] = reads[h][:, :W]
         lq_ref[h] = lhs_of(jnp.exp(q_col[:, h : h + 1]) * query[h].astype(F32) - reads[h][:, W:])
@@ -300,7 +314,7 @@
             raw_ref, v_ref, beta_ref, decay_ref, keys_ref, tf_ref, x_ref, in_copy(1).wait
         )
         pl.semaphore_wait(barrier, 2 * (LINE - 1) + ROWS - 1 + 3)
-        for h in range(HEADS):
+        for h in (1, 0, 2, 3):
             keep = owner & (z == 2 * h + 1)
 
             @pl.when(jnp.logical_not(keep))
@@ -555,7 +569,7 @@
             pltpu.VMEM((inner, outer), BF16),
             pltpu.VMEM((MICRO, inner), BF16),
             pltpu.VMEM((HEADS, 2) + square, F32),
-            pltpu.VMEM((HEADS, 2 * MICRO, 4 * W), BF16),
+            pltpu.VMEM((HEADS, MICRO, 2 * W), F32),
             pltpu.VMEM((HEADS,) + square, F32),
             pltpu.VMEM((HEADS, W, 2 * W), BF16),
             pltpu.VMEM((W, inner), F32),

time: 54 us -> 52.9 us (0.980)
  Pallas kernels: 52.2 us -> 50.7 us
    pallas_call x1, Pallas kernels: 52.2 us -> 50.7 us  [on_device(): pl.pallas_call(layer_kernel, name='layer', out_shape=jax.ShapeDtypeStruct...]
where the time goes in v5:
time: 52.9 us; the launch traced here: 52.3 us
  Pallas kernels  50.7 us (96%)
  local copies, waits for them, and re-layouts  1.57 us (3%)
    pallas_call x1, Pallas kernels, on_device(): pl.pallas_call(layer_kernel, name='layer', out_shape=jax.ShapeDtypeStruct...  50.7 us
    unnamed x1, local copies, waits for them, and re-layouts  1.57 us

profile of v5, /device:TPU:7, one launch (start us, length us, event | category | flops | bytes accessed | tf_op | source)
XLA Modules:
  0.0 52.3 jit_solution(15549370880178626386)
XLA Ops:
  0.0 50.7 %layer.1 = bf16[16,4096]{1,0:T(8,128)(2,1)} custom-call(bf16[128,512]{1,0:T(8,128)(2,1)} %q_hbm.1, bf16[3,128,512]{2,1,0:T(8,128)(2,1)} %bitcast.3, bf16[3,128,512]{2,1,0:T(8,128)(2,1)} %bitcast.4, bf16[128,512]{1,0:T(8,128)(2,1)} %gate_hbm.1, f32[3,4,128]{2,1,0:T(4,128)} %beta_ref.1, f32[4,128]{1,0:T(4,128)} %decay_ref.1, f32[1,128]{1,0:T(1,128)} %bitcast.5, ...), custom_call_target="tpu_custom_call" | custom-call | tf_op jit(solution)/shard_map/layer/pallas_call | solution.py:558
  50.7 1.6 %copy.10 = bf16[16,4096]{1,0:T(8,128)(2,1)} copy(bf16[16,4096]{1,0:T(8,128)(2,1)} %layer.1) | data formatting | bytes 262144

commit v6 on v5

--- a/solution.py
+++ b/solution.py
@@ -278,10 +278,11 @@
             send_sem=start_send.at[to], recv_sem=start_recv.at[h], **at(line + to, served),
         )
 
-    def pair_copy(c):
+    def pair_copy(c, kind):
+        part = pl.ds(0, 1) if kind == 0 else pl.ds(1, RING - 1)
         return pltpu.make_async_remote_copy(
-            src_ref=pair_out.at[c], dst_ref=pair_in.at[c],
-            send_sem=pair_send.at[c], recv_sem=pair_recv.at[c], **at(seq, sibling),
+            src_ref=pair_out.at[c, part], dst_ref=pair_in.at[c, part],
+            send_sem=pair_send.at[kind, c], recv_sem=pair_recv.at[kind, c], **at(seq, sibling),
         )
 
     def ring_copy(kind, c, src, dst, upward):
@@ -291,15 +292,15 @@
         )
 
     def relay_copy(c):
-        return ring_copy(0, c, own_ref.at[c, 2], relay_in.at[c], c < CHUNKS // 2)
+        return ring_copy(0, c, own_ref.at[c, 0], relay_in.at[c], c < CHUNKS // 2)
 
     def side_copy(c):
         part = c // (CHUNKS // 2)
-        return ring_copy(1, c, own_ref.at[c, 3 - 2 * part], side_in.at[1 - part, c], part == 1)
+        return ring_copy(1, c, own_ref.at[c, 3 - part], side_in.at[1 - part, c], part == 1)
 
     def onward_copy(c):
         part = c // (CHUNKS // 2)
-        return ring_copy(2, c, own_ref.at[c, 1 + 2 * part], side_in.at[part, c], part == 0)
+        return ring_copy(2, c, own_ref.at[c, 2 + part], side_in.at[part, c], part == 0)
 
     def each_chunk(body):
         def step(i, carry):
@@ -365,12 +366,30 @@
             (q23,) = compose([m[3]], m[2])
             (q45,) = compose([m[5]], m[4])
             (q67,) = compose([m[7]], m[6])
-            p2, p3 = compose([m[2], q23], p1)
-            q46, q47 = compose([m[6], q67], q45)
-            p4, p5, p6, p7 = compose([m[4], q45, q46, q47], p3)
+            (p3,) = compose([q23], p1)
+            (q47,) = compose([q67], q45)
+            (p7,) = compose([q47], p3)
             total_ref[0] = p7[0]
             total_ref[1] = p7[1]
-            for i, (t, f) in enumerate((m[0], p1, p2, p3, p4, p5, p6, p7)):
+
+            @pl.when(x == 0)
+            def _():
+                for i, to in enumerate((3, 1, 2)):
+                    line_copy(total_ref.at[1], line_ref, i, 0, to).start()
+
+            @pl.when(x == 1)
+            def _():
+                for i, to in enumerate((3, 2)):
+                    line_copy(total_ref, far_ref.at[0], i, 1, to).start()
+
+            @pl.when(x == 2)
+            def _():
+                line_copy(total_ref, far_ref.at[1], 0, 2, 3).start()
+
+            (p2,) = compose([m[2]], p1)
+            (q46,) = compose([m[6]], q45)
+            p4, p5, p6 = compose([m[4], q45, q46], p3)
+            for i, (t, f) in enumerate((m[0], p1, p2, p3, p4, p5, p6)):
                 pre_t_ref[i * W : (i + 1) * W] = lhs_of(t)
                 pre_f_ref[i] = f
 
@@ -382,18 +401,7 @@
         def _():
             @pl.when(x == 0)
             def _():
-                for i, to in enumerate((3, 1, 2)):
-                    line_copy(total_ref.at[1], line_ref, i, 0, to).start()
                 given_ref[0] = jnp.zeros((W, W), F32)
-
-            @pl.when(x == 1)
-            def _():
-                for i, to in enumerate((3, 2)):
-                    line_copy(total_ref, far_ref.at[0], i, 1, to).start()
-
-            @pl.when(x == 2)
-            def _():
-                line_copy(total_ref, far_ref.at[1], 0, 2, 3).start()
 
             @pl.when(x > 0)
             def _():
@@ -483,7 +491,7 @@
 
     def run_project():
         w_copy.wait()
-        block = [lax.rem(y + i, RING) * 2 for i in range(RING)]
+        block = [lax.rem(y + i, RING) * 2 for i in (2, 0, 1, 3)]
         rows = jnp.concatenate(
             [gated_ref[b + 1 - core] for b in block] + [gated_ref[b + core] for b in block], axis=0
         )
@@ -492,21 +500,24 @@
             columns = pl.ds(pl.multiple_of(c * width, width), width)
             part = jnp.dot(rows, w_ref[:, columns], preferred_element_type=F32)
             pair_out[c] = part[:64].reshape(RING, 16, width)
-            pair_copy(c).start()
+            pair_copy(c, 0).start()
+            pair_copy(c, 1).start()
             own_ref[c] = part[64:].reshape(RING, 16, width)
 
         each_chunk(project)
 
     def run_ring():
         def begin(c):
-            pair_copy(c).wait_recv()
-            own_ref[c] = own_ref[c] + pair_in[c]
+            pair_copy(c, 0).wait_recv()
+            own_ref[c, 0] = own_ref[c, 0] + pair_in[c, 0]
             relay_copy(c).start()
+            pair_copy(c, 1).wait_recv()
+            own_ref[c, 1:] = own_ref[c, 1:] + pair_in[c, 1:]
             side_copy(c).start()
 
         def forward(c):
             relay_copy(c).wait_recv()
-            block = 1 + 2 * (c // (CHUNKS // 2))
+            block = 2 + c // (CHUNKS // 2)
             own_ref[c, block] = own_ref[c, block] + relay_in[c]
             onward_copy(c).start()
 
@@ -514,7 +525,7 @@
             side_copy(c).wait_recv()
             onward_copy(c).wait_recv()
             columns = pl.ds(pl.multiple_of(c * width, width), width)
-            out_ref[:, columns] = (own_ref[c, 0] + side_in[0, c] + side_in[1, c]).astype(BF16)
+            out_ref[:, columns] = (own_ref[c, 1] + side_in[0, c] + side_in[1, c]).astype(BF16)
 
         each_chunk(begin)
         each_chunk(forward)
@@ -522,7 +533,8 @@
 
     def end_ring():
         def sent(c):
-            pair_copy(c).wait_send()
+            pair_copy(c, 0).wait_send()
+            pair_copy(c, 1).wait_send()
             relay_copy(c).wait_send()
             side_copy(c).wait_send()
             onward_copy(c).wait_send()
@@ -574,8 +586,8 @@
             pltpu.VMEM((HEADS, W, 2 * W), BF16),
             pltpu.VMEM((W, inner), F32),
             pltpu.VMEM((LINE, 2) + square, F32),
-            pltpu.VMEM((LINE * W, 2 * W), BF16),
-            pltpu.VMEM((LINE,) + square, F32),
+            pltpu.VMEM(((LINE - 1) * W, 2 * W), BF16),
+            pltpu.VMEM((LINE - 1,) + square, F32),
             pltpu.VMEM((2,) + square, F32),
             pltpu.VMEM((2, 2) + square, F32),
             pltpu.VMEM(square, F32),
@@ -595,8 +607,8 @@
             dma((3,)),
             dma((LINE,)),
             dma((HEADS,)),
-            dma((CHUNKS,)),
-            dma((CHUNKS,)),
+            dma((2, CHUNKS)),
+            dma((2, CHUNKS)),
             dma((3, CHUNKS)),
             dma((3, CHUNKS)),
         ],

time: 52.9 us -> 52.4 us (level)
  Pallas kernels: 50.7 us -> 50.1 us
    pallas_call x1, Pallas kernels: 50.7 us -> 50.1 us  [on_device(): pl.pallas_call(layer_kernel, name='layer', out_shape=jax.ShapeDtypeStruct...]
where the time goes in v6:
time: 52.4 us; the launch traced here: 51.7 us
  Pallas kernels  50.1 us (96%)
  local copies, waits for them, and re-layouts  1.57 us (3%)
    pallas_call x1, Pallas kernels, on_device(): pl.pallas_call(layer_kernel, name='layer', out_shape=jax.ShapeDtypeStruct...  50.1 us
    unnamed x1, local copies, waits for them, and re-layouts  1.57 us

profile of v6, /device:TPU:7, one launch (start us, length us, event | category | flops | bytes accessed | tf_op | source)
XLA Modules:
  0.0 51.7 jit_solution(6760288937122907378)
XLA Ops:
  0.0 50.1 %layer.1 = bf16[16,4096]{1,0:T(8,128)(2,1)} custom-call(bf16[128,512]{1,0:T(8,128)(2,1)} %q_hbm.1, bf16[3,128,512]{2,1,0:T(8,128)(2,1)} %bitcast.3, bf16[3,128,512]{2,1,0:T(8,128)(2,1)} %bitcast.4, bf16[128,512]{1,0:T(8,128)(2,1)} %gate_hbm.1, f32[3,4,128]{2,1,0:T(4,128)} %beta_ref.1, f32[4,128]{1,0:T(4,128)} %decay_ref.1, f32[1,128]{1,0:T(1,128)} %bitcast.5, ...), custom_call_target="tpu_custom_call" | custom-call | tf_op jit(solution)/shard_map/layer/pallas_call | solution.py:570
  50.1 1.6 %copy.10 = bf16[16,4096]{1,0:T(8,128)(2,1)} copy(bf16[16,4096]{1,0:T(8,128)(2,1)} %layer.1) | data formatting | bytes 262144

commit v7 on v6

--- a/solution.py
+++ b/solution.py
@@ -252,10 +252,15 @@
 
     barrier = pltpu.get_barrier_semaphore()
     for i in range(1, LINE):
-        for h in (head, sibling):
-            pl.semaphore_signal(barrier, inc=1, **at(line + lax.rem(z + i, LINE), h))
-    for i in range(1, ROWS):
-        pl.semaphore_signal(barrier, inc=1, **at(lax.rem(x + i, ROWS) * LINE + z, head))
+        pl.semaphore_signal(barrier, inc=1, **at(line + lax.rem(z + i, LINE), owners))
+
+    @pl.when(owner)
+    def _():
+        for i in range(1, LINE):
+            pl.semaphore_signal(barrier, inc=1, **at(line + lax.rem(z + i, LINE), sibling))
+        for i in range(1, ROWS):
+            pl.semaphore_signal(barrier, inc=1, **at(lax.rem(x + i, ROWS) * LINE + z, head))
+
     for h in (up, down, sibling):
         pl.semaphore_signal(barrier, inc=1, **at(seq, h))
 
@@ -314,7 +319,7 @@
         held["rows"] = local_maps(
             raw_ref, v_ref, beta_ref, decay_ref, keys_ref, tf_ref, x_ref, in_copy(1).wait
         )
-        pl.semaphore_wait(barrier, 2 * (LINE - 1) + ROWS - 1 + 3)
+        pl.semaphore_wait(barrier, LINE - 1 + 3 + core * (LINE - 1 + ROWS - 1))
         for h in (1, 0, 2, 3):
             keep = owner & (z == 2 * h + 1)
 

time: 52.4 us -> 52.5 us (level)
  the two profiles are of different devices: /device:TPU:7 before, /device:TPU:134 now
where the time goes in v7:
time: 52.5 us; the launch traced here: 52.3 us
  Pallas kernels  50.7 us (97%)
  local copies, waits for them, and re-layouts  1.57 us (3%)
    pallas_call x1, Pallas kernels, on_device(): pl.pallas_call(layer_kernel, name='layer', out_shape=jax.ShapeDtypeStruct...  50.7 us
    unnamed x1, local copies, waits for them, and re-layouts  1.57 us

profile of v7, /device:TPU:134, one launch (start us, length us, event | category | flops | bytes accessed | tf_op | source)
XLA Modules:
  0.0 52.3 jit_solution(17987705280732758602)
XLA Ops:
  0.0 50.7 %layer.1 = bf16[16,4096]{1,0:T(8,128)(2,1)} custom-call(bf16[128,512]{1,0:T(8,128)(2,1)} %q_hbm.1, bf16[3,128,512]{2,1,0:T(8,128)(2,1)} %bitcast.3, bf16[3,128,512]{2,1,0:T(8,128)(2,1)} %bitcast.4, bf16[128,512]{1,0:T(8,128)(2,1)} %gate_hbm.1, f32[3,4,128]{2,1,0:T(4,128)} %beta_ref.1, f32[4,128]{1,0:T(4,128)} %decay_ref.1, f32[1,128]{1,0:T(1,128)} %bitcast.5, ...), custom_call_target="tpu_custom_call" | custom-call | tf_op jit(solution)/shard_map/layer/pallas_call | solution.py:575
  50.7 1.6 %copy.10 = bf16[16,4096]{1,0:T(8,128)(2,1)} copy(bf16[16,4096]{1,0:T(8,128)(2,1)} %layer.1) | data formatting | bytes 262144
